TPU v7x, 32 devices: a whole 2x2x4 slice. The times are simulated.
32 devices in a mesh: tile: 8 (over z, y), band: 4 (over x, core).
Axes of the slice: x: 2, y: 2, z: 4, core: 2. Of those that a mesh axis runs over, the one named last changes fastest.
Arguments:
- sky_model: bfloat16 [4, 16384, 128], P('band', 'tile'), may hold values from -6 to 6
- observed: bfloat16 [4, 8, 1024, 128], P('band', 'tile'), may hold values from -6 to 6
- row_weight: float32 [4, 8, 128], P('band', 'tile'), may hold values from 0.1 to 1
- foot_owner: int32 [4, 8, 1024, 1], P('band', 'tile'), may hold values from 0 to 7; in each aligned block of 1024 rows (0 to 1023, 1024 to 2047, ..., all dimensions but the last counted through in order) at most 256 rows name the same one
- foot_local: int32 [4, 8, 1024], P('band', 'tile'), may hold values from 0 to 2047
- row_offset: int32 [4, 8], P('band', 'tile'), may hold values from -4 to 4
- exposure_of: int32 [4, 8], P('band', 'tile'), may hold values from 0 to 255
- amplitude: float32 [4, 256], replicated, may hold values from 0.25 to 1
- subpixel_shift: float32 [256], replicated, may hold values from 0.05 to 0.95
- column_profile: float32 [256, 4, 25], replicated, may hold values from 0.05 to 0.3
- row_profile: float32 [256, 4, 25], replicated, may hold values from 0.05 to 0.3
Outputs:
- grad_sky: float32 [4, 16384, 128], P('band', 'tile')
- grad_params: float32 [5, 256], replicated
Inputs may be any that keep to these rules, and one draw needn't show every extreme that they name: `foot_owner`: in each aligned block of 1024 columns (the columns of one device's row blocks) no owner index appears more than 256 times, and some owner appears exactly 256 times in some blocks.
All inputs are finite; a program needn't handle non-finite values.
Results may differ from a plain program's by a relative error of at most 0.006.
Values may be sent and summed in bfloat16 or wider, within the bound.
A program may use at most 64 MiB of HBM per device.

v0:
```python
import jax
import jax.numpy as jnp
from jax import lax
from jax.sharding import PartitionSpec as P


def band_lookup(profile, lag_shift, size):
    taps = profile.shape[-1]
    out_index = jnp.arange(size, dtype=jnp.int32)[:, None]
    in_index = jnp.arange(size, dtype=jnp.int32)[None, :]
    lag = in_index - out_index + taps // 2 + lag_shift
    tap_mask = (lag[:, :, None] == jnp.arange(taps, dtype=jnp.int32)[None, None, :]).astype(
        jnp.bfloat16
    )
    return jnp.einsum(
        "vwt,bqt->bqvw", tap_mask, profile, preferred_element_type=jnp.float32
    ).astype(jnp.bfloat16)


def from_previous(values):
    blank = jnp.zeros_like(values[:, :, :1])
    return jnp.concatenate([blank, values[:, :, :-1]], axis=2)


def from_next(values):
    blank = jnp.zeros_like(values[:, :, :1])
    return jnp.concatenate([values[:, :, 1:], blank], axis=2)


def strict_lower(size):
    above = jnp.arange(size, dtype=jnp.int32)[:, None]
    below = jnp.arange(size, dtype=jnp.int32)[None, :]
    return (below < above).astype(jnp.bfloat16)


def body(
    sky_model,
    observed,
    row_weight,
    foot_owner,
    foot_local,
    row_offset,
    exposure_of,
    amplitude,
    subpixel_shift,
    column_profile,
    row_profile,
):
    tile_count = lax.axis_size("tile")
    seg_count = sky_model.shape[1]
    block_rows = sky_model.shape[2]
    block_count = observed.shape[1]
    width = observed.shape[2]
    capacity = 2 * block_count * width // tile_count
    expo_count = amplitude.shape[1]
    comp_count = amplitude.shape[0]
    tile_blocks = width // block_rows
    requests = block_count * width
    pixels = width * block_rows
    highest = lax.Precision.HIGHEST
    bfloat = jnp.bfloat16
    single = jnp.float32
    request_owner = foot_owner.reshape(requests)
    request_local = foot_local.reshape(requests)
    owner_hits = (
        request_owner.reshape(block_count, width)[:, :, None]
        == jnp.arange(tile_count, dtype=jnp.int32)[None, None, :]
    )
    owner_onehot = owner_hits.astype(bfloat)
    within = jnp.einsum(
        "uy,byt->but", strict_lower(width), owner_onehot, preferred_element_type=single
    )
    block_totals = jnp.sum(owner_onehot.astype(single), axis=1)
    before = jnp.dot(strict_lower(block_count).astype(single), block_totals, precision=highest)
    rank_table = jnp.where(owner_hits, within + before[:, None, :], jnp.zeros((), single))
    owner_rank = jnp.sum(rank_table, axis=2).astype(jnp.int32).reshape(requests)
    slot_index = request_owner * capacity + owner_rank
    empty_ids = jnp.zeros((tile_count * capacity,), jnp.int32)
    request_ids = empty_ids.at[slot_index].set(request_local + 1).reshape(tile_count, capacity)
    block_offset = row_offset.reshape(block_count)
    block_exposure = exposure_of.reshape(block_count)
    served_ids = lax.all_to_all(request_ids, "tile", split_axis=0, concat_axis=0, tiled=True)
    served_valid = served_ids > 0
    served_where = jnp.maximum(served_ids - 1, 0)
    local_sky = sky_model[0]
    picked_rows = jnp.take(local_sky, served_where.reshape(tile_count * capacity), axis=0)
    picked_rows = jnp.where(
        served_valid.reshape(tile_count * capacity)[:, None],
        picked_rows,
        jnp.zeros_like(picked_rows),
    )
    served_rows = picked_rows.reshape(tile_count, capacity, block_rows)
    returned = lax.all_to_all(served_rows, "tile", split_axis=0, concat_axis=0, tiled=True)
    fetched = jnp.take(
        returned.reshape(tile_count * capacity, block_rows), slot_index, axis=0
    ).reshape(block_count, width, block_rows)
    expo_onehot = (
        block_exposure[:, None] == jnp.arange(expo_count, dtype=jnp.int32)[None, :]
    ).astype(single)
    block_amp = jnp.dot(expo_onehot, amplitude.T, precision=highest)
    block_frac = jnp.dot(expo_onehot, subpixel_shift, precision=highest)
    block_wide = jnp.einsum("be,eqt->bqt", expo_onehot, column_profile, precision=highest)
    block_tall = jnp.einsum("be,eqt->bqt", expo_onehot, row_profile, precision=highest)
    j_index = jnp.arange(block_rows, dtype=jnp.int32)[None, :, None]
    v_index = jnp.arange(block_rows, dtype=jnp.int32)[None, None, :]
    offsets = block_offset[:, None, None]
    lower_hit = j_index == v_index + offsets
    upper_hit = j_index == v_index + offsets + 1
    zero_b = jnp.zeros((), bfloat)
    weight_low = (1.0 - block_frac).astype(bfloat)[:, None, None]
    weight_high = block_frac.astype(bfloat)[:, None, None]
    interp = jnp.where(lower_hit, weight_low, zero_b) + jnp.where(upper_hit, weight_high, zero_b)
    slope_map = upper_hit.astype(bfloat) - lower_hit.astype(bfloat)
    tall_kernel = band_lookup(block_tall.astype(bfloat), 0, block_rows)
    wide_profile_b = block_wide.astype(bfloat)
    wide_main = band_lookup(wide_profile_b, 0, block_rows)
    wide_prev = band_lookup(wide_profile_b, -block_rows, block_rows)
    wide_next = band_lookup(wide_profile_b, block_rows, block_rows)
    resampled = jnp.einsum("buj,bjv->buv", fetched, interp, preferred_element_type=single).astype(
        bfloat
    )
    blurred = jnp.einsum(
        "buw,bqvw->bquv", resampled, tall_kernel, preferred_element_type=single
    ).astype(bfloat)
    blurred_tiles = blurred.reshape(block_count, comp_count, tile_blocks, block_rows, block_rows)
    component = jnp.einsum(
        "bqxy,bqiyv->bqixv", wide_main, blurred_tiles, preferred_element_type=single
    )
    component = component + from_previous(
        jnp.einsum("bqxy,bqiyv->bqixv", wide_prev, blurred_tiles, preferred_element_type=single)
    )
    component = component + from_next(
        jnp.einsum("bqxy,bqiyv->bqixv", wide_next, blurred_tiles, preferred_element_type=single)
    )
    component = component.reshape(block_count, comp_count, width, block_rows)
    model = jnp.sum(block_amp[:, :, None, None] * component, axis=1)
    weighted = row_weight.reshape(block_count, block_rows)[:, None, :] * (
        model - observed[0].astype(single)
    )
    amp_term = jnp.sum(component * weighted[:, None], axis=(2, 3)) / pixels
    residual_b = weighted.astype(bfloat)
    residual_tiles = residual_b.reshape(block_count, tile_blocks, block_rows, block_rows)
    back_wide = jnp.einsum(
        "bqyx,biyv->bqixv", wide_main, residual_tiles, preferred_element_type=single
    )
    back_wide = back_wide + from_next(
        jnp.einsum("bqyx,biyv->bqixv", wide_prev, residual_tiles, preferred_element_type=single)
    )
    back_wide = back_wide + from_previous(
        jnp.einsum("bqyx,biyv->bqixv", wide_next, residual_tiles, preferred_element_type=single)
    )
    back_wide = back_wide.reshape(block_count, comp_count, width, block_rows).astype(bfloat)
    image_adjoint = jnp.sum(
        block_amp[:, :, None, None]
        * jnp.einsum("bquv,bqvw->bquw", back_wide, tall_kernel, preferred_element_type=single),
        axis=1,
    )
    adjoint_b = image_adjoint.astype(bfloat)
    slope = jnp.einsum("buj,bjv->buv", fetched, slope_map, preferred_element_type=single)
    shift_term = jnp.sum(image_adjoint * slope, axis=(1, 2)) / pixels
    block_terms = jnp.concatenate([amp_term, shift_term[:, None]], axis=1)
    partial_params = jnp.dot(block_terms.T, expo_onehot, precision=highest)
    segment_grad = jnp.einsum("buv,bjv->buj", adjoint_b, interp, preferred_element_type=single)
    send_grad = (
        jnp.zeros((tile_count * capacity, block_rows), single)
        .at[slot_index]
        .set(segment_grad.reshape(requests, block_rows))
        .reshape(tile_count, capacity, block_rows)
    )
    segment_rows = lax.all_to_all(
        send_grad.astype(jnp.bfloat16), "tile", split_axis=0, concat_axis=0, tiled=True
    ).astype(send_grad.dtype)
    flat_rows = segment_rows.reshape(tile_count * capacity, block_rows)
    flat_rows = jnp.where(
        served_valid.reshape(tile_count * capacity)[:, None], flat_rows, jnp.zeros_like(flat_rows)
    )
    grad_local = (
        jnp.zeros((seg_count, block_rows), single)
        .at[served_where.reshape(tile_count * capacity)]
        .add(flat_rows)
    )
    grad_params = lax.psum(partial_params, ("tile", "band"))
    return (grad_local[None], grad_params)


def solution(mesh):
    placed = (
        P("band", "tile", None),
        P("band", "tile", None, None),
        P("band", "tile", None),
        P("band", "tile", None, None),
        P("band", "tile", None),
        P("band", "tile"),
        P("band", "tile"),
        P(),
        P(),
        P(),
        P(),
    )
    return jax.shard_map(
        body, mesh=mesh, in_specs=placed, out_specs=(P("band", "tile", None), P()), check_vma=False
    )
```

profile of v0, /device:TPU:0, one launch (start us, length us, event | category | flops | bytes accessed | tf_op | source)
XLA Modules:
  0.0 138.0 jit_solution(9144185370389907575)
XLA Ops:
  0.7 0.9 convert_reduce_fusion
  1.5 1.5 %fusion.17 = f32[1024]{0:T(1024)S(1)} fusion(s32[1024]{0:T(1024)} %bitcast.184, f32[8]{0:T(128)S(1)} %broadcast_multiply_fusion.1), kind=kOutput, calls=%fused_computation.38 | convolution fusion | flops 17873920 | bytes 8224 | tf_op jit(solution)/shard_map/uy,byt->but/dot_general | solution.py:70
  4.5 4.9 %scatter_custom_fusion = s32[2048]{0:T(1024)} fusion(s32[1024]{0:T(1024)S(1)} %bitcast.189, s32[1024]{0:T(1024)S(1)} %bitcast.193, s32[]{:T(128)} %constant.24.clone.1), kind=kCustom, calls=%fused_computation.120 | custom fusion | bytes 8196 | tf_op jit(solution)/shard_map/scatter | solution.py:79
  9.4 7.3 %all-to-all-start = ((s32[8,1,256]{2,1,0:T(1,128)}), s32[8,1,256]{2,1,0:T(1,128)S(1)}, u32[]{:S(2)}, u32[]{:S(2)}) async-start(s32[8,1,256]{2,1,0:T(1,128)} %bitcast.7), calls=%async_computation | async-start | bytes 16384 | tf_op jit(solution)/shard_map/all_to_all | solution.py:82
  18.0 1.1 fusion.45
  21.9 1.3 all-to-all-done
  23.2 6.2 %gather_fusion = bf16[2048,128]{1,0:T(8,128)(2,1)S(1)} fusion(bf16[2048,128]{1,0:T(8,128)(2,1)S(1)} %bitcast.168, s32[2048]{0:T(1024)S(1)} %broadcast_clamp_fusion), kind=kCustom, calls=%fused_computation | custom fusion | bytes 1056768 | tf_op jit(solution)/shard_map/jit(_take)/gather | solution.py:86
  29.4 1.4 %select_select_fusion = bf16[8,256,128]{2,1,0:T(8,128)(2,1)} fusion(bf16[8,256,128]{2,1,0:T(8,128)(2,1)S(1)} %bitcast.174, pred[8,256]{1,0:T(8,128)(4,1)S(1)} %get-tuple-element.3, pred[8,256]{1,0:T(8,128)(4,1)S(1)} %bitcast.188), kind=kLoop, calls=%fused_computation.51 | loop fusion | flops 524288 | bytes 1052672 | tf_op jit(solution)/shard_map/jit(_where)/select_n | solution.py:87
  30.9 4.7 %all-to-all-start.1 = ((bf16[8,256,128]{2,1,0:T(8,128)(2,1)}), bf16[8,256,128]{2,1,0:T(8,128)(2,1)S(1)}, u32[]{:S(2)}, u32[]{:S(2)}) async-start(bf16[8,256,128]{2,1,0:T(8,128)(2,1)} %select_select_fusion), calls=%async_computation.1 | async-start | bytes 1048576 | tf_op jit(solution)/shard_map/all_to_all | solution.py:93
  37.3 1.0 copy.63
  41.9 7.6 %all-to-all-done.1 = bf16[8,256,128]{2,1,0:T(8,128)(2,1)S(1)} async-done(((bf16[8,256,128]{2,1,0:T(8,128)(2,1)}), bf16[8,256,128]{2,1,0:T(8,128)(2,1)S(1)}, u32[]{:S(2)}, u32[]{:S(2)}) %all-to-all-start.1) | async-done | bytes 524320 | tf_op jit(solution)/shard_map/all_to_all | solution.py:93
  49.5 3.2 %gather_fusion.1 = bf16[1024,128]{1,0:T(8,128)(2,1)S(1)} fusion(bf16[2048,128]{1,0:T(8,128)(2,1)S(1)} %bitcast.172, s32[1024]{0:T(1024)S(1)} %broadcast_clamp_fusion.1), kind=kCustom, calls=%fused_computation.1 | custom fusion | bytes 528384 | tf_op jit(solution)/shard_map/jit(_take)/gather | solution.py:94
  56.0 1.0 copy.72
  57.0 2.0 %subtract_multiply_fusion = f32[1,1,1024,128]{3,2,1,0:T(8,128)} fusion(f32[1,1,1024,128]{3,2,1,0:T(8,128)} %bitcast.176, f32[128]{0:T(128)} %bitcast.198, bf16[1,1,1024,128]{3,2,1,0:T(8,128)(2,1)} %param.12), kind=kLoop, calls=%fused_computation.49 | loop fusion | flops 393216 | bytes 1311232 | tf_op jit(solution)/shard_map/mul | solution.py:137
  59.0 2.0 %copy.73 = f32[8,128,128]{1,2,0:T(8,128)} copy(f32[8,128,128]{2,1,0:T(8,128)} %bitcast.175) | data formatting | bytes 1048576 | tf_op jit(solution)/shard_map/mul | solution.py:140
  61.0 1.2 fusion.32
  66.7 0.8 copy-done.1
  67.7 4.1 %scatter_custom_fusion.1 = f32[2048,128]{1,0:T(8,128)} fusion(s32[1024]{0:T(1024)S(1)} %bitcast.191, f32[1024,128]{1,0:T(8,128)S(1)} %fusion.36, f32[]{:T(128)} %constant.23.clone.1), kind=kCustom, calls=%fused_computation.55 | custom fusion | bytes 1048580 | tf_op jit(solution)/shard_map/scatter | solution.py:167
  71.8 2.1 %convert_element_type.210 = bf16[2048,128]{1,0:T(8,128)(2,1)} convert(f32[2048,128]{1,0:T(8,128)} %scatter_custom_fusion.1) | non-fusion elementwise | flops 262144 | bytes 1572864 | tf_op jit(solution)/shard_map/convert_element_type | solution.py:171
  73.9 3.8 %all-to-all-start.2 = ((bf16[8,256,128]{2,1,0:T(8,128)(2,1)}), bf16[8,256,128]{2,1,0:T(8,128)(2,1)S(1)}, u32[]{:S(2)}, u32[]{:S(2)}) async-start(bf16[8,256,128]{2,1,0:T(8,128)(2,1)} %bitcast.52), calls=%async_computation.2 | async-start | bytes 1048576 | tf_op jit(solution)/shard_map/all_to_all | solution.py:170
  77.7 2.0 %fusion.25 = f32[]{:T(128)} fusion(f32[1024,128]{1,0:T(8,128)} %copy-done.1, bf16[1024,128]{1,0:T(8,128)(2,1)S(1)} %gather_fusion.1, pred[1024]{0:T(1024)(128)(4,1)S(1)} %compare_and_fusion, s32[128]{0:T(128)S(1)} %copy-done.14, s32[128]{0:T(128)S(1)} %copy-done.12), kind=kOutput, calls=%fused_computation.48 | convolution fusion | flops 34078720 | bytes 788484 | tf_op jit(solution)/shard_map/buj,bjv->buv/dot_general | solution.py:159
  80.3 1.4 multiply_reduce_fusion
  81.9 41.1 %psum.7 = f32[5,256]{1,0:T(8,128)} all-reduce(f32[5,256]{1,0:T(8,128)S(1)} %broadcast_multiply_fusion), channel_id=1, replica_groups=mesh['tile'=8,'band'=4] {'tile','band'}, use_global_device_ids=true, to_apply=%region_9.10 | all-reduce | flops 1280 | bytes 10240 | tf_op jit(solution)/shard_map/psum | solution.py:182
  123.3 14.6 %scatter_custom_fusion.2 = f32[2048,128]{1,0:T(8,128)} fusion(s32[2048]{0:T(1024)S(1)} %bitcast.187, f32[2048,128]{1,0:T(8,128)S(1)} %convert_select_fusion, f32[]{:T(128)} %constant.23.clone.1), kind=kCustom, calls=%fused_computation.53 | custom fusion | flops 262144 | bytes 1048580 | tf_op jit(solution)/shard_map/scatter-add | solution.py:180
  (88 shorter events, 16.7 us)
Async XLA Ops:
  0.6 22.6 %copy-start = (bf16[1,2048,128]{2,1,0:T(8,128)(2,1)S(1)}, bf16[1,2048,128]{2,1,0:T(8,128)(2,1)}, u32[]{:S(2)}) copy-start(bf16[1,2048,128]{2,1,0:T(8,128)(2,1)} %param.11) | copy-start | bytes 1572868
  0.6 19.9 %copy-start.16 = (f32[256]{0:T(256)S(1)}, f32[256]{0:T(256)}, u32[]{:S(2)}) copy-start(f32[256]{0:T(256)} %param.19) | copy-start | bytes 3076
  0.7 20.5 %copy-start.19 = (f32[4,256]{1,0:T(4,128)S(1)}, f32[4,256]{1,0:T(4,128)}, u32[]{:S(2)}) copy-start(f32[4,256]{1,0:T(4,128)} %param.18) | copy-start | bytes 12292
  9.4 13.8 %all-to-all-start = ((s32[8,1,256]{2,1,0:T(1,128)}), s32[8,1,256]{2,1,0:T(1,128)S(1)}, u32[]{:S(2)}, u32[]{:S(2)}) async-start(s32[8,1,256]{2,1,0:T(1,128)} %bitcast.7), calls=%async_computation | async-start | bytes 16384 | tf_op jit(solution)/shard_map/all_to_all | solution.py:82
  21.9 30.9 %copy-start.11 = (s32[128]{0:T(128)}, s32[128]{0:T(128)S(1)}, u32[]{:S(2)}) copy-start(s32[128]{0:T(128)S(1)} %get-tuple-element.6) | copy-start | bytes 1540
  21.9 30.9 %copy-start.13 = (s32[128]{0:T(128)}, s32[128]{0:T(128)S(1)}, u32[]{:S(2)}) copy-start(s32[128]{0:T(128)S(1)} %get-tuple-element.7) | copy-start | bytes 1540
  29.4 7.9 %copy-start.2 = (bf16[1,1,1024,128]{3,2,1,0:T(8,128)(2,1)S(1)}, bf16[1,1,1024,128]{3,2,1,0:T(8,128)(2,1)}, u32[]{:S(2)}) copy-start(bf16[1,1,1024,128]{3,2,1,0:T(8,128)(2,1)} %param.12) | copy-start | bytes 786436
  29.4 11.2 %copy-start.9 = (s32[1,1,1024,1]{2,3,1,0:T(1,128)S(1)}, s32[1,1,1024,1]{2,3,1,0:T(1,128)}, u32[]{:S(2)}) copy-start(s32[1,1,1024,1]{2,3,1,0:T(1,128)} %param.14) | copy-start | bytes 12292
  29.4 11.2 %copy-start.6 = (f32[256,4,25]{0,1,2:T(4,128)S(1)}, f32[256,4,25]{0,1,2:T(4,128)}, u32[]{:S(2)}) copy-start(f32[256,4,25]{0,1,2:T(4,128)} %param.21) | copy-start | bytes 307204
  30.9 18.7 %all-to-all-start.1 = ((bf16[8,256,128]{2,1,0:T(8,128)(2,1)}), bf16[8,256,128]{2,1,0:T(8,128)(2,1)S(1)}, u32[]{:S(2)}, u32[]{:S(2)}) async-start(bf16[8,256,128]{2,1,0:T(8,128)(2,1)} %select_select_fusion), calls=%async_computation.1 | async-start | bytes 1048576 | tf_op jit(solution)/shard_map/all_to_all | solution.py:93
  41.3 12.4 %copy-start.7 = (bf16[4,128,128]{2,0,1:T(4,128)(2,1)}, bf16[4,128,128]{2,0,1:T(4,128)(2,1)S(1)}, u32[]{:S(2)}) copy-start(bf16[4,128,128]{2,0,1:T(4,128)(2,1)S(1)} %fusion.11) | copy-start | bytes 393220
  54.8 0.7 copy-start.17
  57.0 5.2 %copy-start.5 = (bf16[4,128,128]{1,2,0:T(8,128)(2,1)S(1)}, bf16[4,128,128]{1,2,0:T(8,128)(2,1)}, u32[]{:S(2)}) copy-start(bf16[4,128,128]{1,2,0:T(8,128)(2,1)} %copy.67) | copy-start | bytes 393220
  62.7 0.9 copy-start.4
  64.0 0.9 copy-start.3
  65.3 0.9 copy-start.8
  65.4 0.9 copy-start.18
  65.4 2.1 %copy-start.12 = (s32[128]{0:T(128)S(1)}, s32[128]{0:T(128)}, u32[]{:S(2)}) copy-start(s32[128]{0:T(128)} %copy-done.11) | copy-start | bytes 1540
  65.4 2.1 %copy-start.14 = (s32[128]{0:T(128)S(1)}, s32[128]{0:T(128)}, u32[]{:S(2)}) copy-start(s32[128]{0:T(128)} %copy-done.13) | copy-start | bytes 1540
  66.7 0.8 copy-start.1
  73.9 7.9 %copy-start.15 = (f32[1,256]{1,0:T(1,128)S(1)}, f32[1,256]{1,0:T(1,128)}, u32[]{:S(2)}) copy-start(f32[1,256]{1,0:T(1,128)} %compare_convert_fusion) | copy-start | bytes 3076
  73.9 49.1 %copy-start.10 = (pred[2048]{0:T(1024)(128)(4,1)S(1)}, pred[2048]{0:T(1024)(128)(4,1)}, u32[]{:S(2)}) copy-start(pred[2048]{0:T(1024)(128)(4,1)} %gt.15) | copy-start | bytes 6148
  73.9 49.1 %all-to-all-start.2 = ((bf16[8,256,128]{2,1,0:T(8,128)(2,1)}), bf16[8,256,128]{2,1,0:T(8,128)(2,1)S(1)}, u32[]{:S(2)}, u32[]{:S(2)}) async-start(bf16[8,256,128]{2,1,0:T(8,128)(2,1)} %bitcast.52), calls=%async_computation.2 | async-start | bytes 1048576 | tf_op jit(solution)/shard_map/all_to_all | solution.py:170
where the time goes:
time: 139 us; the launch traced here: 138 us
  blocking collectives  41.1 us (30%)
  local copies, waits for them, and re-layouts  29.9 us (22%)
  other arithmetic  26.7 us (19%)
  starting transfers between devices  15.8 us (11%)
  matrix products  11.5 us (8%)
  waiting for transfers between devices  8.93 us (6%)
  between operations  4.1 us (3%)
    psum x1, blocking collectives, body(): grad_params = lax.psum(partial_params, ('tile', 'band'))  41.1 us
    scatter-add x1, other arithmetic, body(): grad_local = jnp.zeros((seg_count, block_rows), single).at[served_where.r...  14.6 us
    all_to_all x1, waiting for transfers between devices, body(): lax.all_to_all(served_rows, 'tile', split_axis=0, concat_axis=0, tiled=True)  7.62 us
    all_to_all x1, starting transfers between devices, body(): lax.all_to_all(request_ids, 'tile', split_axis=0, concat_axis=0, tiled=True)  7.28 us
    gather x1, local copies, waits for them, and re-layouts, body(): jnp.take(local_sky, served_where.reshape(tile_count * capacity), axis=0)  6.18 us
    scatter x1, local copies, waits for them, and re-layouts, body(): empty_ids.at[slot_index].set(request_local + 1)  4.88 us
    all_to_all x1, starting transfers between devices, body(): lax.all_to_all(served_rows, 'tile', split_axis=0, concat_axis=0, tiled=True)  4.71 us
    scatter x1, local copies, waits for them, and re-layouts, body(): send_grad = jnp.zeros((tile_count * capacity, block_rows), single).at[slo...  4.07 us
  transfers between devices with their start and end apart: 3, of which 2 were waited for; matrix products, arithmetic and copies ran while one was open for 9% of the time, Pallas kernels for 0%

commit v1 on v0

v1 whole, which is shorter than its diff:
```python
import functools

import jax
import jax.numpy as jnp
from jax import lax
from jax.experimental import pallas as pl
from jax.experimental.pallas import tpu as pltpu
from jax.sharding import PartitionSpec as P

MESH = pl.DeviceIdType.MESH
BF = jnp.bfloat16
F32 = jnp.float32
TN = (((0,), (0,)), ((), ()))
NT = (((1,), (1,)), ((), ()))


def iota(shape, dim):
    return lax.broadcasted_iota(jnp.int32, shape, dim)


def dot(a, b):
    return jnp.dot(a, b, preferred_element_type=F32)


def onehot(hit):
    return jnp.where(hit, 1.0, 0.0).astype(BF)


def bands(taps_b, rev):
    comps, taps = taps_b.shape
    place_t = iota((taps, 256), 0)
    place_m = iota((taps, 256), 1) - (128 - taps // 2)
    place = onehot(place_m == ((taps - 1 - place_t) if rev else place_t))
    base = dot(taps_b, place)
    x = jnp.concatenate(
        [jnp.broadcast_to(base[q : q + 1], (128, 256)) for q in range(comps)], axis=0
    )
    row = iota(x.shape, 0)
    for bit in range(7):
        x = jnp.where((row & (1 << bit)) != 0, pltpu.roll(x, 1 << bit, 1), x)
    return x


def kernel(
    tiles,
    nband,
    cap,
    owner_ref,
    local_ref,
    weight_ref,
    offset_ref,
    expo_ref,
    amp_ref,
    frac_ref,
    sky_hbm,
    obs_hbm,
    col_hbm,
    rowp_hbm,
    grad_ref,
    params_ref,
    sky,
    obs,
    colp,
    rowp,
    hits,
    picks,
    req_out,
    req_in,
    rows_out,
    rows_in,
    grads_out,
    grads_in,
    terms_out,
    terms_in,
    part_out,
    part_in,
    fet,
    blur,
    fwd,
    bwd,
    tall,
    tall_t,
    obs_t,
    resid,
    comp,
    back,
    seg_grad,
    total,
    load_sem,
    req_s,
    req_r,
    rows_s,
    rows_r,
    grads_s,
    grads_r,
    terms_s,
    terms_r,
    part_s,
    part_r,
):
    me = lax.axis_index("tile")
    band = lax.axis_index("band")
    segs, rows = sky.shape
    width = obs.shape[0]
    comps = blur.shape[0]
    pixels = width * rows
    nblk = width // 256

    loads = [
        pltpu.make_async_copy(src, dst, load_sem.at[i])
        for i, (src, dst) in enumerate(
            ((sky_hbm, sky), (obs_hbm, obs), (col_hbm, colp), (rowp_hbm, rowp))
        )
    ]
    for load in loads:
        load.start()

    barrier = pltpu.get_barrier_semaphore()

    def greet_tile(k, c):
        pl.semaphore_signal(
            barrier, inc=1, device_id={"tile": lax.rem(me + 1 + k, tiles)}, device_id_type=MESH
        )
        return c

    def greet_band(k, c):
        pl.semaphore_signal(
            barrier, inc=1, device_id={"band": lax.rem(band + 1 + k, nband)}, device_id_type=MESH
        )
        return c

    lax.fori_loop(0, tiles - 1, greet_tile, 0)
    lax.fori_loop(0, nband - 1, greet_band, 0)

    def after(k):
        return lax.rem(me + 1 + k, tiles)

    def ahead(k):
        return lax.rem(me + (tiles - 1) - k, tiles)

    def push(src, dst, send, recv, p):
        return pltpu.make_async_remote_copy(
            src_ref=src.at[p],
            dst_ref=dst.at[me],
            send_sem=send.at[p],
            recv_sem=recv.at[me],
            device_id={"tile": p},
            device_id_type=MESH,
        )

    def arrival(src, dst, send, recv, p):
        return pltpu.make_async_remote_copy(
            src_ref=src.at[p],
            dst_ref=dst.at[p],
            send_sem=send.at[p],
            recv_sem=recv.at[p],
            device_id={"tile": p},
            device_id_type=MESH,
        )

    owner = owner_ref[...]
    member = jnp.where(iota((tiles, width), 0) == owner, 1.0, 0.0)
    pieces = [member[:, b * 128 : (b + 1) * 128] for b in range(width // 128)]
    above = onehot(iota((128, 128), 0) < iota((128, 128), 1))
    prefix = dot(jnp.concatenate(pieces, axis=0).astype(BF), above)
    run = jnp.zeros((tiles, 1), F32)
    ranks = []
    for b, piece in enumerate(pieces):
        earlier = prefix[b * tiles : (b + 1) * tiles] + run
        ranks.append(jnp.sum(piece * earlier, axis=0, keepdims=True))
        run = run + jnp.sum(piece, axis=1, keepdims=True)
    slot = owner * cap + jnp.concatenate(ranks, axis=1).astype(jnp.int32)
    wanted = local_ref[...] + 1
    which = iota((16, width), 0)
    digits = (
        jnp.where(which == 0, wanted >> 6, jnp.where(which == 1, wanted & 63, 0))
        .astype(F32)
        .astype(BF)
    )

    pl.semaphore_wait(barrier, tiles - 1 + nband - 1)

    def ask(p, out):
        hit = onehot(iota((cap, width), 0) + p * cap == slot)
        hits[p] = hit
        ids = lax.dot_general(digits, hit, NT, preferred_element_type=F32)
        out[p] = ids[0:1] * 64.0 + ids[1:2]

    def ask_peer(k, c):
        p = after(k)
        ask(p, req_out)
        push(req_out, req_in, req_s, req_r, p).start()
        return c

    lax.fori_loop(0, tiles - 1, ask_peer, 0)
    ask(me, req_in)
    loads[0].wait()

    def serve(p):
        ids = jnp.broadcast_to(req_in[p], (128, cap)).T
        lane = iota((cap, 128), 1).astype(F32)
        for b in range(segs // 128):
            picks[p, :, b * 128 : (b + 1) * 128] = onehot(ids == lane + float(b * 128 + 1))
        rows_out[p] = dot(picks[p], sky[...]).astype(BF)

    def serve_peer(k, c):
        p = ahead(k)
        arrival(req_out, req_in, req_s, req_r, p).wait_recv()
        serve(p)
        push(rows_out, rows_in, rows_s, rows_r, p).start()
        return c

    lax.fori_loop(0, tiles - 1, serve_peer, 0)
    serve(me)

    for load in loads[1:]:
        load.wait()
    expo = expo_ref[0, 0]
    offset = offset_ref[0, 0]
    amps = [amp_ref[q, expo] for q in range(comps)]
    col_b = colp[expo].astype(BF)
    row_b = rowp[expo].astype(BF)
    low = iota((128, 128), 1) < 64
    for rev, wide in ((True, fwd), (False, bwd)):
        made = bands(col_b, rev)
        zero = jnp.zeros((128, 128), F32)
        for q in range(comps):
            edge = made[q * 128 : (q + 1) * 128, :128]
            mid = made[q * 128 : (q + 1) * 128, 128:].astype(BF)
            left = jnp.where(low, 0.0, edge).astype(BF)
            right = jnp.where(low, edge, 0.0).astype(BF)
            none = zero.astype(BF)
            line = [none, left, mid, right, none, none]
            for b in range(4):
                for h in range(2):
                    at = h + 3 - b
                    at = at if 0 <= at < 6 else 0
                    wide[q, b * 128 : (b + 1) * 128, h * 128 : (h + 1) * 128] = line[at]
    made = bands(row_b, False)
    for q in range(comps):
        tall[q * 128 : (q + 1) * 128, :] = made[q * 128 : (q + 1) * 128, 128:].astype(BF)
    made = bands(row_b, True)
    for q in range(comps):
        tall_t[:, q * 128 : (q + 1) * 128] = made[q * 128 : (q + 1) * 128, 128:].astype(BF)
    for b in range(width // 128):
        i, h = b // 2, b % 2
        obs_t[i * 128 : (i + 1) * 128, h * 128 : (h + 1) * 128] = (
            obs[b * 128 : (b + 1) * 128, :].astype(F32).T
        )
    heavy = jnp.broadcast_to(weight_ref[...], (128, 128)).T
    frac = jnp.full((128, 128), frac_ref[expo], F32)
    w_low = (1.0 - frac).astype(BF).astype(F32)
    w_high = frac.astype(BF).astype(F32)
    sub, lane = iota((128, 128), 0), iota((128, 128), 1)
    interp_t = (
        jnp.where(lane == sub + offset, w_low, 0.0)
        + jnp.where(lane == sub + offset + 1, w_high, 0.0)
    ).astype(BF)
    interp = (
        jnp.where(sub == lane + offset, w_low, 0.0)
        + jnp.where(sub == lane + offset + 1, w_high, 0.0)
    ).astype(BF)
    slope_t = (
        jnp.where(lane == sub + offset + 1, 1.0, 0.0) - jnp.where(lane == sub + offset, 1.0, 0.0)
    ).astype(BF)
    blank = jnp.zeros((128, 128), BF)
    for q in range(comps):
        blur[q, :, :128] = blank
        blur[q, :, 128 + width :] = blank
    resid[:, :128] = blank
    resid[:, 128 + width :] = blank

    fet[...] = lax.dot_general(rows_out[me], hits[me], TN, preferred_element_type=F32)

    def take(k, c):
        p = after(k)
        arrival(rows_out, rows_in, rows_s, rows_r, p).wait_recv()
        fet[...] += lax.dot_general(rows_in[p], hits[p], TN, preferred_element_type=F32)
        return c

    lax.fori_loop(0, tiles - 1, take, 0)

    fetched = fet[...].astype(BF)
    resampled = dot(interp_t, fetched).astype(BF)
    for q in range(comps):
        blur[q, :, 128 : 128 + width] = dot(tall[q * 128 : (q + 1) * 128, :], resampled).astype(BF)
    model = None
    for q in range(comps):
        left = jnp.concatenate([blur[q, :, i * 256 : i * 256 + 512] for i in range(nblk)], axis=0)
        part = dot(left, fwd[q])
        comp[q] = part
        model = amps[q] * part if model is None else model + amps[q] * part
    scale = jnp.concatenate([jnp.concatenate([heavy, heavy], axis=1)] * nblk, axis=0)
    weighted = scale * (model - obs_t[...])
    terms = [
        jnp.sum(jnp.sum(comp[q] * weighted, axis=0, keepdims=True), axis=1, keepdims=True) / pixels
        for q in range(comps)
    ]
    weighted_b = weighted.astype(BF)
    for i in range(nblk):
        resid[:, 128 + i * 256 : 128 + (i + 1) * 256] = weighted_b[i * 128 : (i + 1) * 128]
    left = jnp.concatenate([resid[:, i * 256 : i * 256 + 512] for i in range(nblk)], axis=0)
    for q in range(comps):
        back[q] = (amps[q] * dot(left, bwd[q])).astype(BF)
    shift = jnp.zeros((128, 256), F32)
    for i in range(nblk):
        stack = jnp.concatenate(
            [back[q, i * 128 : (i + 1) * 128, :] for q in range(comps)], axis=0
        )
        adjoint = dot(tall_t[...], stack)
        shift = shift + adjoint * dot(slope_t, fetched[:, i * 256 : (i + 1) * 256])
        seg_grad[i * 256 : (i + 1) * 256, :] = dot(interp, adjoint.astype(BF)).T.astype(BF)
    terms.append(jnp.sum(jnp.sum(shift, axis=0, keepdims=True), axis=1, keepdims=True) / pixels)

    line = iota((8, 128), 0)
    card = jnp.where(line == 5, expo.astype(F32), 0.0)
    for q, term in enumerate(terms):
        card = jnp.where(line == q, jnp.broadcast_to(term, (8, 128)), card)
    terms_out[...] = card
    terms_in[me] = card

    def tell(p):
        return pltpu.make_async_remote_copy(
            src_ref=terms_out,
            dst_ref=terms_in.at[me],
            send_sem=terms_s.at[p],
            recv_sem=terms_r.at[me],
            device_id={"tile": p},
            device_id_type=MESH,
        )

    def tell_peer(k, c):
        tell(after(k)).start()
        return c

    lax.fori_loop(0, tiles - 1, tell_peer, 0)

    def give(p):
        grads_out[p] = dot(hits[p], seg_grad[...]).astype(BF)

    def give_peer(k, c):
        p = after(k)
        give(p)
        push(grads_out, grads_in, grads_s, grads_r, p).start()
        return c

    lax.fori_loop(0, tiles - 1, give_peer, 0)
    give(me)

    def hear(k, c):
        p = ahead(k)
        pltpu.make_async_remote_copy(
            src_ref=terms_out,
            dst_ref=terms_in.at[p],
            send_sem=terms_s.at[p],
            recv_sem=terms_r.at[p],
            device_id={"tile": p},
            device_id_type=MESH,
        ).wait_recv()
        return c

    lax.fori_loop(0, tiles - 1, hear, 0)
    expos = params_ref.shape[1]
    column = iota((8, 128), 1).astype(F32)

    def gather_terms(t, acc):
        block = terms_in[t]
        named = block[5:6, :]
        return tuple(
            a + jnp.where(column + float(128 * b) == named, block, 0.0) for b, a in enumerate(acc)
        )

    acc = lax.fori_loop(
        0,
        tiles,
        gather_terms,
        tuple(jnp.zeros((8, 128), F32) for _ in range(expos // 128)),
    )
    whole = jnp.concatenate(acc, axis=1)
    part_out[...] = whole
    part_in[band] = whole

    def share(k, here):
        to = lax.rem(band + 1 + k, nband)
        return pltpu.make_async_remote_copy(
            src_ref=part_out,
            dst_ref=part_in.at[band] if here else part_in.at[to],
            send_sem=part_s.at[to],
            recv_sem=part_r.at[band] if here else part_r.at[to],
            device_id={"band": to},
            device_id_type=MESH,
        )

    for k in range(nband - 1):
        share(k, True).start()

    total[...] = lax.dot_general(grads_out[me], picks[me], TN, preferred_element_type=F32)

    def collect(k, c):
        p = ahead(k)
        arrival(grads_out, grads_in, grads_s, grads_r, p).wait_recv()
        total[...] += lax.dot_general(grads_in[p], picks[p], TN, preferred_element_type=F32)
        return c

    lax.fori_loop(0, tiles - 1, collect, 0)
    for b in range(segs // 128):
        grad_ref[b * 128 : (b + 1) * 128, :] = total[:, b * 128 : (b + 1) * 128].T

    for k in range(nband - 1):
        share(k, False).wait_recv()
    summed = part_in[0]
    for b in range(1, nband):
        summed = summed + part_in[b]
    params_ref[...] = summed[: comps + 1]

    def settle(k, c):
        p = after(k)
        push(req_out, req_in, req_s, req_r, p).wait_send()
        push(rows_out, rows_in, rows_s, rows_r, p).wait_send()
        push(grads_out, grads_in, grads_s, grads_r, p).wait_send()
        tell(p).wait_send()
        return c

    lax.fori_loop(0, tiles - 1, settle, 0)
    for k in range(nband - 1):
        share(k, True).wait_send()


def body(
    sky_model,
    observed,
    row_weight,
    foot_owner,
    foot_local,
    row_offset,
    exposure_of,
    amplitude,
    subpixel_shift,
    column_profile,
    row_profile,
):
    tiles = lax.axis_size("tile")
    nband = lax.axis_size("band")
    segs, rows = sky_model.shape[1:]
    width = observed.shape[2]
    comps, expos = amplitude.shape
    taps = column_profile.shape[2]
    cap = 2 * width // tiles
    vmem = pl.BlockSpec(memory_space=pltpu.VMEM)
    smem = pl.BlockSpec(memory_space=pltpu.SMEM)
    hbm = pl.BlockSpec(memory_space=pl.ANY)
    dma = pltpu.SemaphoreType.DMA
    grad, params = pl.pallas_call(
        functools.partial(kernel, tiles, nband, cap),
        out_shape=(
            jax.ShapeDtypeStruct((segs, rows), F32),
            jax.ShapeDtypeStruct((comps + 1, expos), F32),
        ),
        in_specs=[vmem, vmem, vmem, smem, smem, smem, smem, hbm, hbm, hbm, hbm],
        out_specs=(vmem, vmem),
        scratch_shapes=[
            pltpu.VMEM((segs, rows), BF),
            pltpu.VMEM((width, rows), BF),
            pltpu.VMEM((expos, comps, taps), F32),
            pltpu.VMEM((expos, comps, taps), F32),
            pltpu.VMEM((tiles, cap, width), BF),
            pltpu.VMEM((tiles, cap, segs), BF),
            pltpu.VMEM((tiles, 1, cap), F32),
            pltpu.VMEM((tiles, 1, cap), F32),
            pltpu.VMEM((tiles, cap, rows), BF),
            pltpu.VMEM((tiles, cap, rows), BF),
            pltpu.VMEM((tiles, cap, rows), BF),
            pltpu.VMEM((tiles, cap, rows), BF),
            pltpu.VMEM((8, 128), F32),
            pltpu.VMEM((tiles, 8, 128), F32),
            pltpu.VMEM((8, expos), F32),
            pltpu.VMEM((nband, 8, expos), F32),
            pltpu.VMEM((rows, width), F32),
            pltpu.VMEM((comps, rows, width + 256), BF),
            pltpu.VMEM((comps, 512, 256), BF),
            pltpu.VMEM((comps, 512, 256), BF),
            pltpu.VMEM((comps * rows, rows), BF),
            pltpu.VMEM((rows, comps * rows), BF),
            pltpu.VMEM((width // 256 * rows, 256), F32),
            pltpu.VMEM((rows, width + 256), BF),
            pltpu.VMEM((comps, width // 256 * rows, 256), F32),
            pltpu.VMEM((comps, width // 256 * rows, 256), BF),
            pltpu.VMEM((width, rows), BF),
            pltpu.VMEM((rows, segs), F32),
            dma((4,)),
        ]
        + [dma((tiles,))] * 8
        + [dma((nband,))] * 2,
        compiler_params=pltpu.CompilerParams(
            collective_id=0, has_side_effects=True, vmem_limit_bytes=52 * 1024 * 1024
        ),
    )(
        foot_owner.reshape(1, width),
        foot_local.reshape(1, width),
        row_weight.reshape(1, rows),
        row_offset,
        exposure_of,
        amplitude,
        subpixel_shift,
        sky_model[0],
        observed[0, 0],
        column_profile,
        row_profile,
    )
    return (grad[None], params)


def solution(mesh):
    placed = (
        P("band", "tile", None),
        P("band", "tile", None, None),
        P("band", "tile", None),
        P("band", "tile", None, None),
        P("band", "tile", None),
        P("band", "tile"),
        P("band", "tile"),
        P(),
        P(),
        P(),
        P(),
    )
    return jax.shard_map(
        body, mesh=mesh, in_specs=placed, out_specs=(P("band", "tile", None), P()), check_vma=False
    )
```

time: 139 us -> 47.2 us (0.34)
  the two profiles are of different devices: /device:TPU:0 before, /device:TPU:13 now
where the time goes in v1:
time: 47.2 us; the launch traced here: 47 us
  Pallas kernels  40 us (85%)
  local copies, waits for them, and re-layouts  4.98 us (11%)
  between operations  2.04 us (4%)
    pallas_call x1, Pallas kernels, body(): pl.pallas_call(functools.partial(kernel, tiles, nband, cap), out_shape=(j...  40 us
    unnamed x20, local copies, waits for them, and re-layouts  4.98 us

profile of v1, /device:TPU:13, one launch (start us, length us, event | category | flops | bytes accessed | tf_op | source)
XLA Modules:
  0.0 47.0 jit_solution(5390128512848583511)
XLA Ops:
  1.9 0.0 copy-start.7
  1.9 0.0 copy-start
  1.9 1.2 %copy.13.col_hbm = f32[256,4,25]{2,1,0:T(4,128)S(1)} copy(f32[256,4,25]{0,1,2:T(4,128)} %param.20) | data formatting | bytes 204800 | tf_op args[9]
  3.2 0.0 copy-done.7
  3.2 0.0 copy-start.1
  3.2 0.0 copy-start.2
  3.2 0.0 copy-start.3
  3.2 0.0 copy-start.4
  3.2 0.0 copy-start.5
  3.2 0.0 copy-start.6
  3.2 0.3 copy.14.rowp_hbm
  3.5 0.0 copy-done
  3.5 0.6 %copy-done.1 = bf16[1,1,1024,128]{3,2,1,0:T(8,128)(2,1)S(1)} copy-done((bf16[1,1,1024,128]{3,2,1,0:T(8,128)(2,1)S(1)}, bf16[1,1,1024,128]{3,2,1,0:T(8,128)(2,1)}, u32[]{:S(2)}) %copy-start.1) | copy-done | bytes 262168
  4.1 0.0 copy-done.2
  4.1 0.0 copy-done.3
  4.1 0.0 copy-done.4
  4.1 0.0 copy-done.5
  4.1 0.0 copy-done.6
  4.1 40.0 %shard_map.122 = (f32[2048,128]{1,0:T(8,128)}, f32[5,256]{1,0:T(8,128)S(1)}) custom-call(s32[1,1024]{1,0:T(1,128)S(1)} %bitcast.8, s32[1,1024]{1,0:T(1,128)S(1)} %bitcast.9, f32[1,128]{1,0:T(1,128)S(1)} %bitcast.10, s32[1,1]{1,0:T(1,128)S(6)} %copy.17.offset_ref, s32[1,1]{1,0:T(1,128)S(6)} %copy.18.expo_ref, f32[4,256]{1,0:T(4,128)S(1)} %copy-done.4, ...), custom_call_target="tpu_custom_call" | custom-call | tf_op jit(solution)/shard_map/pallas_call | solution.py:453
  44.2 2.3 %copy.19 = f32[1,2048,128]{2,1,0:T(8,128)} copy(f32[1,2048,128]{2,1,0:T(8,128)} %bitcast.11) | data formatting | bytes 2097152
  46.4 0.6 %copy.20 = f32[5,256]{1,0:T(8,128)} copy(f32[5,256]{1,0:T(8,128)S(1)} %get-tuple-element.9) | data formatting | bytes 10240
Async XLA Ops:
  1.9 1.2 %copy-start.7 = (f32[256,4,25]{0,1,2:T(4,128)S(1)}, f32[256,4,25]{0,1,2:T(4,128)}, u32[]{:S(2)}) copy-start(f32[256,4,25]{0,1,2:T(4,128)} %param.21) | copy-start | bytes 307204
  1.9 1.6 %copy-start = (bf16[1,2048,128]{2,1,0:T(8,128)(2,1)S(1)}, bf16[1,2048,128]{2,1,0:T(8,128)(2,1)}, u32[]{:S(2)}) copy-start(bf16[1,2048,128]{2,1,0:T(8,128)(2,1)} %param.11) | copy-start | bytes 1572868
  3.2 1.0 %copy-start.1 = (bf16[1,1,1024,128]{3,2,1,0:T(8,128)(2,1)S(1)}, bf16[1,1,1024,128]{3,2,1,0:T(8,128)(2,1)}, u32[]{:S(2)}) copy-start(bf16[1,1,1024,128]{3,2,1,0:T(8,128)(2,1)} %param.12) | copy-start | bytes 786436
  3.2 0.9 %copy-start.2 = (s32[1,1,1024,1]{2,3,1,0:T(1,128)S(1)}, s32[1,1,1024,1]{2,3,1,0:T(1,128)}, u32[]{:S(2)}) copy-start(s32[1,1,1024,1]{2,3,1,0:T(1,128)} %param.14) | copy-start | bytes 12292
  3.2 0.9 %copy-start.3 = (s32[1,1,1024]{2,1,0:T(1,128)S(1)}, s32[1,1,1024]{2,1,0:T(1,128)}, u32[]{:S(2)}) copy-start(s32[1,1,1024]{2,1,0:T(1,128)} %param.15) | copy-start | bytes 12292
  3.2 0.9 %copy-start.4 = (f32[4,256]{1,0:T(4,128)S(1)}, f32[4,256]{1,0:T(4,128)}, u32[]{:S(2)}) copy-start(f32[4,256]{1,0:T(4,128)} %amp_ref.1) | copy-start | bytes 12292
  3.2 0.9 %copy-start.5 = (f32[256]{0:T(256)S(1)}, f32[256]{0:T(256)}, u32[]{:S(2)}) copy-start(f32[256]{0:T(256)} %frac_ref.1) | copy-start | bytes 3076
  3.2 0.9 %copy-start.6 = (f32[1,1,128]{2,1,0:T(1,128)S(1)}, f32[1,1,128]{2,1,0:T(1,128)}, u32[]{:S(2)}) copy-start(f32[1,1,128]{2,1,0:T(1,128)} %param.13) | copy-start | bytes 1540

commit v2 on v1

--- a/solution.py
+++ b/solution.py
@@ -26,12 +26,20 @@
     return jnp.where(hit, 1.0, 0.0).astype(BF)
 
 
-def bands(taps_b, rev):
-    comps, taps = taps_b.shape
-    place_t = iota((taps, 256), 0)
-    place_m = iota((taps, 256), 1) - (128 - taps // 2)
-    place = onehot(place_m == ((taps - 1 - place_t) if rev else place_t))
-    base = dot(taps_b, place)
+def spread(ref, expo):
+    taps, comps, expos = ref.shape
+    named = iota((comps, expos), 1) == expo
+    lane = iota((comps, 256), 1) - (128 - taps // 2)
+    straight = mirrored = jnp.zeros((comps, 256), F32)
+    for t in range(taps):
+        tap = jnp.sum(jnp.where(named, ref[t], 0.0), axis=1, keepdims=True)
+        straight = jnp.where(lane == t, tap, straight)
+        mirrored = jnp.where(lane == taps - 1 - t, tap, mirrored)
+    return straight.astype(BF).astype(F32), mirrored.astype(BF).astype(F32)
+
+
+def bands(base):
+    comps = base.shape[0]
     x = jnp.concatenate(
         [jnp.broadcast_to(base[q : q + 1], (128, 256)) for q in range(comps)], axis=0
     )
@@ -39,6 +47,14 @@
     for bit in range(7):
         x = jnp.where((row & (1 << bit)) != 0, pltpu.roll(x, 1 << bit, 1), x)
     return x
+
+
+def steps(low, high, work):
+    if high - low <= 8:
+        for k in range(low, high):
+            work(k)
+    else:
+        lax.fori_loop(low, high, lambda k, c: (work(k), c)[1], 0)
 
 
 def kernel(
@@ -56,8 +72,8 @@
     obs_hbm,
     col_hbm,
     rowp_hbm,
-    grad_ref,
-    params_ref,
+    total,
+    summed_ref,
     sky,
     obs,
     colp,
@@ -70,8 +86,8 @@
     rows_in,
     grads_out,
     grads_in,
-    terms_out,
-    terms_in,
+    card_out,
+    cards,
     part_out,
     part_in,
     fet,
@@ -82,10 +98,10 @@
     tall_t,
     obs_t,
     resid,
-    comp,
+    back_f,
     back,
+    adj,
     seg_grad,
-    total,
     load_sem,
     req_s,
     req_r,
@@ -93,8 +109,8 @@
     rows_r,
     grads_s,
     grads_r,
-    terms_s,
-    terms_r,
+    cards_s,
+    cards_r,
     part_s,
     part_r,
 ):
@@ -132,11 +148,9 @@
     lax.fori_loop(0, tiles - 1, greet_tile, 0)
     lax.fori_loop(0, nband - 1, greet_band, 0)
 
-    def after(k):
-        return lax.rem(me + 1 + k, tiles)
-
-    def ahead(k):
-        return lax.rem(me + (tiles - 1) - k, tiles)
+    def peer(k):
+        bits = [1 << b for b in range(tiles.bit_length() - 1)]
+        return sum(lax.rem(me // bit + k // bit, 2) * bit for bit in bits)
 
     def push(src, dst, send, recv, p):
         return pltpu.make_async_remote_copy(
@@ -186,14 +200,13 @@
         ids = lax.dot_general(digits, hit, NT, preferred_element_type=F32)
         out[p] = ids[0:1] * 64.0 + ids[1:2]
 
-    def ask_peer(k, c):
-        p = after(k)
+    def ask_peer(k):
+        p = peer(k)
         ask(p, req_out)
         push(req_out, req_in, req_s, req_r, p).start()
-        return c
-
-    lax.fori_loop(0, tiles - 1, ask_peer, 0)
-    ask(me, req_in)
+
+    half = tiles // 2
+    steps(half, tiles, ask_peer)
     loads[0].wait()
 
     def serve(p):
@@ -203,14 +216,20 @@
             picks[p, :, b * 128 : (b + 1) * 128] = onehot(ids == lane + float(b * 128 + 1))
         rows_out[p] = dot(picks[p], sky[...]).astype(BF)
 
-    def serve_peer(k, c):
-        p = ahead(k)
+    def serve_peer(k):
+        p = peer(k)
         arrival(req_out, req_in, req_s, req_r, p).wait_recv()
         serve(p)
         push(rows_out, rows_in, rows_s, rows_r, p).start()
-        return c
-
-    lax.fori_loop(0, tiles - 1, serve_peer, 0)
+
+    def both(k):
+        ask_peer(k)
+        serve_peer(half + k - 1)
+
+    steps(1, half, both)
+    serve_peer(tiles - 1)
+    steps(1, half, serve_peer)
+    ask(me, req_in)
     serve(me)
 
     for load in loads[1:]:
@@ -218,11 +237,11 @@
     expo = expo_ref[0, 0]
     offset = offset_ref[0, 0]
     amps = [amp_ref[q, expo] for q in range(comps)]
-    col_b = colp[expo].astype(BF)
-    row_b = rowp[expo].astype(BF)
+    col, col_mirror = spread(colp, expo)
+    row, row_mirror = spread(rowp, expo)
     low = iota((128, 128), 1) < 64
-    for rev, wide in ((True, fwd), (False, bwd)):
-        made = bands(col_b, rev)
+    for base, wide in ((col_mirror, fwd), (col, bwd)):
+        made = bands(base)
         zero = jnp.zeros((128, 128), F32)
         for q in range(comps):
             edge = made[q * 128 : (q + 1) * 128, :128]
@@ -236,10 +255,10 @@
                     at = h + 3 - b
                     at = at if 0 <= at < 6 else 0
                     wide[q, b * 128 : (b + 1) * 128, h * 128 : (h + 1) * 128] = line[at]
-    made = bands(row_b, False)
+    made = bands(row)
     for q in range(comps):
         tall[q * 128 : (q + 1) * 128, :] = made[q * 128 : (q + 1) * 128, 128:].astype(BF)
-    made = bands(row_b, True)
+    made = bands(row_mirror)
     for q in range(comps):
         tall_t[:, q * 128 : (q + 1) * 128] = made[q * 128 : (q + 1) * 128, 128:].astype(BF)
     for b in range(width // 128):
@@ -272,158 +291,147 @@
 
     fet[...] = lax.dot_general(rows_out[me], hits[me], TN, preferred_element_type=F32)
 
-    def take(k, c):
-        p = after(k)
+    def take(k):
+        p = peer(k)
         arrival(rows_out, rows_in, rows_s, rows_r, p).wait_recv()
         fet[...] += lax.dot_general(rows_in[p], hits[p], TN, preferred_element_type=F32)
-        return c
-
-    lax.fori_loop(0, tiles - 1, take, 0)
+
+    steps(half, tiles - 2, take)
+    steps(1, half, take)
+    steps(tiles - 2, tiles, take)
 
     fetched = fet[...].astype(BF)
     resampled = dot(interp_t, fetched).astype(BF)
     for q in range(comps):
-        blur[q, :, 128 : 128 + width] = dot(tall[q * 128 : (q + 1) * 128, :], resampled).astype(BF)
+        blur[q, :, 128 : 128 + width] = (
+            amps[q] * dot(tall[q * 128 : (q + 1) * 128, :], resampled)
+        ).astype(BF)
     model = None
     for q in range(comps):
         left = jnp.concatenate([blur[q, :, i * 256 : i * 256 + 512] for i in range(nblk)], axis=0)
         part = dot(left, fwd[q])
-        comp[q] = part
-        model = amps[q] * part if model is None else model + amps[q] * part
+        model = part if model is None else model + part
     scale = jnp.concatenate([jnp.concatenate([heavy, heavy], axis=1)] * nblk, axis=0)
-    weighted = scale * (model - obs_t[...])
-    terms = [
-        jnp.sum(jnp.sum(comp[q] * weighted, axis=0, keepdims=True), axis=1, keepdims=True) / pixels
-        for q in range(comps)
-    ]
-    weighted_b = weighted.astype(BF)
+    weighted_b = (scale * (model - obs_t[...])).astype(BF)
     for i in range(nblk):
         resid[:, 128 + i * 256 : 128 + (i + 1) * 256] = weighted_b[i * 128 : (i + 1) * 128]
     left = jnp.concatenate([resid[:, i * 256 : i * 256 + 512] for i in range(nblk)], axis=0)
     for q in range(comps):
-        back[q] = (amps[q] * dot(left, bwd[q])).astype(BF)
-    shift = jnp.zeros((128, 256), F32)
+        part = amps[q] * dot(left, bwd[q])
+        back_f[q] = part
+        back[q] = part.astype(BF)
     for i in range(nblk):
         stack = jnp.concatenate(
             [back[q, i * 128 : (i + 1) * 128, :] for q in range(comps)], axis=0
         )
         adjoint = dot(tall_t[...], stack)
-        shift = shift + adjoint * dot(slope_t, fetched[:, i * 256 : (i + 1) * 256])
+        adj[:, i * 256 : (i + 1) * 256] = adjoint
         seg_grad[i * 256 : (i + 1) * 256, :] = dot(interp, adjoint.astype(BF)).T.astype(BF)
-    terms.append(jnp.sum(jnp.sum(shift, axis=0, keepdims=True), axis=1, keepdims=True) / pixels)
+
+    def give(p):
+        grads_out[p] = dot(hits[p], seg_grad[...]).astype(BF)
+
+    def give_peer(k):
+        p = peer(k)
+        give(p)
+        push(grads_out, grads_in, grads_s, grads_r, p).start()
+
+    steps(half, tiles, give_peer)
+
+    terms = []
+    for q in range(comps):
+        acc = jnp.zeros((128, 256), F32)
+        for i in range(nblk):
+            acc = acc + (
+                blur[q, :, 128 + i * 256 : 128 + (i + 1) * 256].astype(F32)
+                * back_f[q, i * 128 : (i + 1) * 128, :]
+            )
+        acc = jnp.sum(jnp.sum(acc, axis=0, keepdims=True), axis=1, keepdims=True)
+        gain = jnp.full((1, 1), amps[q], F32)
+        terms.append(acc / (gain * gain * pixels))
+    shift = jnp.sum(adj[...] * dot(slope_t, fetched), axis=0, keepdims=True)
+    terms.append(jnp.sum(shift, axis=1, keepdims=True) / pixels)
 
     line = iota((8, 128), 0)
     card = jnp.where(line == 5, expo.astype(F32), 0.0)
     for q, term in enumerate(terms):
         card = jnp.where(line == q, jnp.broadcast_to(term, (8, 128)), card)
-    terms_out[...] = card
-    terms_in[me] = card
-
-    def tell(p):
+    card_out[...] = card
+    cards[band] = card
+
+    def swap(src, dst, send, recv, k, here):
+        to = lax.rem(band + 1 + k, nband)
         return pltpu.make_async_remote_copy(
-            src_ref=terms_out,
-            dst_ref=terms_in.at[me],
-            send_sem=terms_s.at[p],
-            recv_sem=terms_r.at[me],
+            src_ref=src,
+            dst_ref=dst.at[band] if here else dst.at[to],
+            send_sem=send.at[to],
+            recv_sem=recv.at[band] if here else recv.at[to],
+            device_id={"band": to},
+            device_id_type=MESH,
+        )
+
+    for k in range(nband - 1):
+        swap(card_out, cards, cards_s, cards_r, k, True).start()
+
+    steps(1, half, give_peer)
+    give(me)
+
+    for k in range(nband - 1):
+        swap(card_out, cards, cards_s, cards_r, k, False).wait_recv()
+    expos = summed_ref.shape[1]
+    column = iota((8, expos), 1).astype(F32)
+    part = jnp.zeros((8, expos), F32)
+    for b in range(nband):
+        block = jnp.concatenate([cards[b]] * (expos // 128), axis=1)
+        part = part + jnp.where(column == block[5:6, :], block, 0.0)
+    part_out[...] = part
+    part_in[me] = part
+
+    def tell(p, here):
+        return pltpu.make_async_remote_copy(
+            src_ref=part_out,
+            dst_ref=part_in.at[me] if here else part_in.at[p],
+            send_sem=part_s.at[p],
+            recv_sem=part_r.at[me] if here else part_r.at[p],
             device_id={"tile": p},
             device_id_type=MESH,
         )
 
-    def tell_peer(k, c):
-        tell(after(k)).start()
-        return c
-
-    lax.fori_loop(0, tiles - 1, tell_peer, 0)
-
-    def give(p):
-        grads_out[p] = dot(hits[p], seg_grad[...]).astype(BF)
-
-    def give_peer(k, c):
-        p = after(k)
-        give(p)
-        push(grads_out, grads_in, grads_s, grads_r, p).start()
-        return c
-
-    lax.fori_loop(0, tiles - 1, give_peer, 0)
-    give(me)
-
-    def hear(k, c):
-        p = ahead(k)
-        pltpu.make_async_remote_copy(
-            src_ref=terms_out,
-            dst_ref=terms_in.at[p],
-            send_sem=terms_s.at[p],
-            recv_sem=terms_r.at[p],
-            device_id={"tile": p},
-            device_id_type=MESH,
-        ).wait_recv()
-        return c
-
-    lax.fori_loop(0, tiles - 1, hear, 0)
-    expos = params_ref.shape[1]
-    column = iota((8, 128), 1).astype(F32)
-
-    def gather_terms(t, acc):
-        block = terms_in[t]
-        named = block[5:6, :]
-        return tuple(
-            a + jnp.where(column + float(128 * b) == named, block, 0.0) for b, a in enumerate(acc)
-        )
-
-    acc = lax.fori_loop(
-        0,
-        tiles,
-        gather_terms,
-        tuple(jnp.zeros((8, 128), F32) for _ in range(expos // 128)),
-    )
-    whole = jnp.concatenate(acc, axis=1)
-    part_out[...] = whole
-    part_in[band] = whole
-
-    def share(k, here):
-        to = lax.rem(band + 1 + k, nband)
-        return pltpu.make_async_remote_copy(
-            src_ref=part_out,
-            dst_ref=part_in.at[band] if here else part_in.at[to],
-            send_sem=part_s.at[to],
-            recv_sem=part_r.at[band] if here else part_r.at[to],
-            device_id={"band": to},
-            device_id_type=MESH,
-        )
-
-    for k in range(nband - 1):
-        share(k, True).start()
+    steps(1, tiles, lambda k: tell(peer(k), True).start())
 
     total[...] = lax.dot_general(grads_out[me], picks[me], TN, preferred_element_type=F32)
 
-    def collect(k, c):
-        p = ahead(k)
+    def collect(k):
+        p = peer(k)
         arrival(grads_out, grads_in, grads_s, grads_r, p).wait_recv()
         total[...] += lax.dot_general(grads_in[p], picks[p], TN, preferred_element_type=F32)
-        return c
-
-    lax.fori_loop(0, tiles - 1, collect, 0)
-    for b in range(segs // 128):
-        grad_ref[b * 128 : (b + 1) * 128, :] = total[:, b * 128 : (b + 1) * 128].T
-
-    for k in range(nband - 1):
-        share(k, False).wait_recv()
-    summed = part_in[0]
-    for b in range(1, nband):
-        summed = summed + part_in[b]
-    params_ref[...] = summed[: comps + 1]
-
-    def settle(k, c):
-        p = after(k)
+
+    steps(half, tiles - 2, collect)
+    steps(1, half, collect)
+    steps(tiles - 2, tiles, collect)
+
+    steps(1, tiles, lambda k: tell(peer(k), False).wait_recv())
+    summed_ref[...] = lax.fori_loop(
+        0, tiles, lambda t, acc: acc + part_in[t], jnp.zeros((8, expos), F32)
+    )
+
+    def settle(k):
+        p = peer(k)
         push(req_out, req_in, req_s, req_r, p).wait_send()
         push(rows_out, rows_in, rows_s, rows_r, p).wait_send()
         push(grads_out, grads_in, grads_s, grads_r, p).wait_send()
-        tell(p).wait_send()
-        return c
-
-    lax.fori_loop(0, tiles - 1, settle, 0)
+        tell(p, True).wait_send()
+
+    steps(1, tiles, settle)
     for k in range(nband - 1):
-        share(k, True).wait_send()
+        swap(card_out, cards, cards_s, cards_r, k, True).wait_send()
+
+
+def finish(total, summed, grad_ref, params_ref):
+    rows = grad_ref.shape[0]
+    at = pl.multiple_of(pl.program_id(0) * rows, rows)
+    grad_ref[...] = total[:, pl.ds(at, rows)].T
+    params_ref[...] = summed[: params_ref.shape[0]]
 
 
 def body(
@@ -448,21 +456,21 @@
     cap = 2 * width // tiles
     vmem = pl.BlockSpec(memory_space=pltpu.VMEM)
     smem = pl.BlockSpec(memory_space=pltpu.SMEM)
-    hbm = pl.BlockSpec(memory_space=pl.ANY)
+    hbm = pl.BlockSpec(memory_space=pltpu.HBM)
     dma = pltpu.SemaphoreType.DMA
-    grad, params = pl.pallas_call(
+    total, summed = pl.pallas_call(
         functools.partial(kernel, tiles, nband, cap),
         out_shape=(
-            jax.ShapeDtypeStruct((segs, rows), F32),
-            jax.ShapeDtypeStruct((comps + 1, expos), F32),
+            jax.ShapeDtypeStruct((rows, segs), F32),
+            jax.ShapeDtypeStruct((8, expos), F32),
         ),
         in_specs=[vmem, vmem, vmem, smem, smem, smem, smem, hbm, hbm, hbm, hbm],
         out_specs=(vmem, vmem),
         scratch_shapes=[
             pltpu.VMEM((segs, rows), BF),
             pltpu.VMEM((width, rows), BF),
-            pltpu.VMEM((expos, comps, taps), F32),
-            pltpu.VMEM((expos, comps, taps), F32),
+            pltpu.VMEM((taps, comps, expos), F32),
+            pltpu.VMEM((taps, comps, expos), F32),
             pltpu.VMEM((tiles, cap, width), BF),
             pltpu.VMEM((tiles, cap, segs), BF),
             pltpu.VMEM((tiles, 1, cap), F32),
@@ -472,9 +480,9 @@
             pltpu.VMEM((tiles, cap, rows), BF),
             pltpu.VMEM((tiles, cap, rows), BF),
             pltpu.VMEM((8, 128), F32),
-            pltpu.VMEM((tiles, 8, 128), F32),
+            pltpu.VMEM((nband, 8, 128), F32),
             pltpu.VMEM((8, expos), F32),
-            pltpu.VMEM((nband, 8, expos), F32),
+            pltpu.VMEM((tiles, 8, expos), F32),
             pltpu.VMEM((rows, width), F32),
             pltpu.VMEM((comps, rows, width + 256), BF),
             pltpu.VMEM((comps, 512, 256), BF),
@@ -485,14 +493,15 @@
             pltpu.VMEM((rows, width + 256), BF),
             pltpu.VMEM((comps, width // 256 * rows, 256), F32),
             pltpu.VMEM((comps, width // 256 * rows, 256), BF),
+            pltpu.VMEM((rows, width), F32),
             pltpu.VMEM((width, rows), BF),
-            pltpu.VMEM((rows, segs), F32),
             dma((4,)),
         ]
-        + [dma((tiles,))] * 8
-        + [dma((nband,))] * 2,
+        + [dma((tiles,))] * 6
+        + [dma((nband,))] * 2
+        + [dma((tiles,))] * 2,
         compiler_params=pltpu.CompilerParams(
-            collective_id=0, has_side_effects=True, vmem_limit_bytes=52 * 1024 * 1024
+            collective_id=0, has_side_effects=True, vmem_limit_bytes=36 * 1024 * 1024
         ),
     )(
         foot_owner.reshape(1, width),
@@ -504,9 +513,23 @@
         subpixel_shift,
         sky_model[0],
         observed[0, 0],
-        column_profile,
-        row_profile,
+        column_profile.transpose(2, 1, 0),
+        row_profile.transpose(2, 1, 0),
     )
+    piece = min(512, segs)
+    grad, params = pl.pallas_call(
+        finish,
+        grid=(segs // piece,),
+        out_shape=(
+            jax.ShapeDtypeStruct((segs, rows), F32),
+            jax.ShapeDtypeStruct((comps + 1, expos), F32),
+        ),
+        in_specs=[vmem, vmem],
+        out_specs=(
+            pl.BlockSpec((piece, rows), lambda i: (i, 0)),
+            pl.BlockSpec((comps + 1, expos), lambda i: (0, 0)),
+        ),
+    )(total, summed)
     return (grad[None], params)
 
 

time: 47.2 us -> 54 us (1.14)
  the two profiles are of different devices: /device:TPU:13 before, /device:TPU:0 now
where the time goes in v2:
time: 54 us; the launch traced here: 53.6 us
  Pallas kernels  45.6 us (84%)
  local copies, waits for them, and re-layouts  6.02 us (11%)
  between operations  2.01 us (4%)
    pallas_call x1, Pallas kernels, body(): pl.pallas_call(functools.partial(kernel, tiles, nband, cap), out_shape=(j...  42.6 us
    unnamed x22, local copies, waits for them, and re-layouts  6.02 us
    pallas_call x1, Pallas kernels, body(): pl.pallas_call(finish, grid=(segs // piece,), out_shape=(jax.ShapeDtypeSt...  3.04 us

profile of v2, /device:TPU:0, one launch (start us, length us, event | category | flops | bytes accessed | tf_op | source)
XLA Modules:
  0.0 53.6 jit_solution(8351592721287096873)
XLA Ops:
  1.3 0.0 copy-start.10
  1.9 0.0 copy-start.8
  2.0 0.0 copy-start.7
  2.0 0.0 copy-start.6
  2.0 0.0 copy-start.9
  2.0 0.0 copy-done.10
  2.0 0.6 %copy-done.8 = f32[4,256]{1,0:T(4,128)S(1)} copy-done((f32[4,256]{1,0:T(4,128)S(1)}, f32[4,256]{1,0:T(4,128)}, u32[]{:S(2)}) %copy-start.8) | copy-done | bytes 4120
  2.6 0.0 copy-done.7
  2.7 0.0 copy-done.6
  2.7 0.0 copy-done.9
  2.7 0.0 copy-start.1
  2.7 1.0 %copy-done.1 = bf16[1,2048,128]{2,1,0:T(8,128)(2,1)S(1)} copy-done((bf16[1,2048,128]{2,1,0:T(8,128)(2,1)S(1)}, bf16[1,2048,128]{2,1,0:T(8,128)(2,1)}, u32[]{:S(2)}) %copy-start.1) | copy-done | bytes 524312
  3.7 0.0 copy-start.2
  3.7 0.9 %copy-done.2 = bf16[1,1,1024,128]{3,2,1,0:T(8,128)(2,1)S(1)} copy-done((bf16[1,1,1024,128]{3,2,1,0:T(8,128)(2,1)S(1)}, bf16[1,1,1024,128]{3,2,1,0:T(8,128)(2,1)}, u32[]{:S(2)}) %copy-start.2) | copy-done | bytes 262168
  4.7 0.0 copy-start.3
  4.7 0.9 %copy-done.3 = f32[256,4,25]{0,1,2:T(4,128)S(1)} copy-done((f32[256,4,25]{0,1,2:T(4,128)S(1)}, f32[256,4,25]{0,1,2:T(4,128)}, u32[]{:S(2)}) %copy-start.3) | copy-done | bytes 102424
  5.6 0.0 copy-start.4
  5.6 0.9 %copy-done.4 = f32[256,4,25]{0,1,2:T(4,128)S(1)} copy-done((f32[256,4,25]{0,1,2:T(4,128)S(1)}, f32[256,4,25]{0,1,2:T(4,128)}, u32[]{:S(2)}) %copy-start.4) | copy-done | bytes 102424
  6.5 42.6 %shard_map.122 = (f32[128,2048]{1,0:T(8,128)S(1)}, f32[8,256]{1,0:T(8,128)S(1)}) custom-call(s32[1,1024]{1,0:T(1,128)S(1)} %bitcast.12, s32[1,1024]{1,0:T(1,128)S(1)} %bitcast.13, f32[1,128]{1,0:T(1,128)S(1)} %bitcast.14, s32[1,1]{1,0:T(1,128)S(6)} %copy.13.offset_ref, s32[1,1]{1,0:T(1,128)S(6)} %copy.14.expo_ref, f32[4,256]{1,0:T(4,128)S(1)} %copy-done.8, ...), custom_call_target="tpu_custom_call" | custom-call | tf_op jit(solution)/shard_map/pallas_call | solution.py:461
  49.0 0.0 copy-start
  49.0 1.0 %copy-done = f32[128,2048]{1,0:T(8,128)} copy-done((f32[128,2048]{1,0:T(8,128)}, f32[128,2048]{1,0:T(8,128)S(1)}, u32[]{:S(2)}) %copy-start) | copy-done | bytes 1048600
  50.0 0.0 copy-start.5
  50.0 0.6 %copy-done.5 = f32[8,256]{1,0:T(8,128)} copy-done((f32[8,256]{1,0:T(8,128)}, f32[8,256]{1,0:T(8,128)S(1)}, u32[]{:S(2)}) %copy-start.5) | copy-done | bytes 8216
  50.6 3.0 %shard_map.123 = (f32[2048,128]{1,0:T(8,128)}, f32[5,256]{1,0:T(8,128)}) custom-call(f32[128,2048]{1,0:T(8,128)} %copy-done, f32[8,256]{1,0:T(8,128)} %copy-done.5), custom_call_target="tpu_custom_call" | custom-call | tf_op jit(solution)/shard_map/pallas_call | solution.py:520
Async XLA Ops:
  1.3 0.7 %copy-start.10 = (f32[1,1,128]{2,1,0:T(1,128)S(1)}, f32[1,1,128]{2,1,0:T(1,128)}, u32[]{:S(2)}) copy-start(f32[1,1,128]{2,1,0:T(1,128)} %param.13) | copy-start | bytes 1540
  1.9 0.7 %copy-start.8 = (f32[4,256]{1,0:T(4,128)S(1)}, f32[4,256]{1,0:T(4,128)}, u32[]{:S(2)}) copy-start(f32[4,256]{1,0:T(4,128)} %amp_ref.1) | copy-start | bytes 12292
  2.0 0.7 %copy-start.7 = (s32[1,1,1024]{2,1,0:T(1,128)S(1)}, s32[1,1,1024]{2,1,0:T(1,128)}, u32[]{:S(2)}) copy-start(s32[1,1,1024]{2,1,0:T(1,128)} %param.15) | copy-start | bytes 12292
  2.0 0.7 %copy-start.6 = (s32[1,1,1024,1]{2,3,1,0:T(1,128)S(1)}, s32[1,1,1024,1]{2,3,1,0:T(1,128)}, u32[]{:S(2)}) copy-start(s32[1,1,1024,1]{2,3,1,0:T(1,128)} %param.14) | copy-start | bytes 12292
  2.0 0.7 %copy-start.9 = (f32[256]{0:T(256)S(1)}, f32[256]{0:T(256)}, u32[]{:S(2)}) copy-start(f32[256]{0:T(256)} %frac_ref.1) | copy-start | bytes 3076
  2.7 1.0 %copy-start.1 = (bf16[1,2048,128]{2,1,0:T(8,128)(2,1)S(1)}, bf16[1,2048,128]{2,1,0:T(8,128)(2,1)}, u32[]{:S(2)}) copy-start(bf16[1,2048,128]{2,1,0:T(8,128)(2,1)} %param.11) | copy-start | bytes 1572868
  3.7 0.9 %copy-start.2 = (bf16[1,1,1024,128]{3,2,1,0:T(8,128)(2,1)S(1)}, bf16[1,1,1024,128]{3,2,1,0:T(8,128)(2,1)}, u32[]{:S(2)}) copy-start(bf16[1,1,1024,128]{3,2,1,0:T(8,128)(2,1)} %param.12) | copy-start | bytes 786436
  4.7 0.9 %copy-start.3 = (f32[256,4,25]{0,1,2:T(4,128)S(1)}, f32[256,4,25]{0,1,2:T(4,128)}, u32[]{:S(2)}) copy-start(f32[256,4,25]{0,1,2:T(4,128)} %param.20) | copy-start | bytes 307204
  5.6 0.9 %copy-start.4 = (f32[256,4,25]{0,1,2:T(4,128)S(1)}, f32[256,4,25]{0,1,2:T(4,128)}, u32[]{:S(2)}) copy-start(f32[256,4,25]{0,1,2:T(4,128)} %param.21) | copy-start | bytes 307204
  49.0 1.0 %copy-start = (f32[128,2048]{1,0:T(8,128)}, f32[128,2048]{1,0:T(8,128)S(1)}, u32[]{:S(2)}) copy-start(f32[128,2048]{1,0:T(8,128)S(1)} %get-tuple-element.6.total) | copy-start | bytes 3145732
  50.0 0.6 %copy-start.5 = (f32[8,256]{1,0:T(8,128)}, f32[8,256]{1,0:T(8,128)S(1)}, u32[]{:S(2)}) copy-start(f32[8,256]{1,0:T(8,128)S(1)} %get-tuple-element.7.summed) | copy-start | bytes 24580

commit v3 on v2

v3 whole, which is shorter than its diff:
```python
import functools

import jax
import jax.numpy as jnp
from jax import lax
from jax.experimental import pallas as pl
from jax.experimental.pallas import tpu as pltpu
from jax.sharding import PartitionSpec as P

MESH = pl.DeviceIdType.MESH
BF = jnp.bfloat16
F32 = jnp.float32
TN = (((0,), (0,)), ((), ()))
NT = (((1,), (1,)), ((), ()))


def iota(shape, dim):
    return lax.broadcasted_iota(jnp.int32, shape, dim)


def dot(a, b):
    return jnp.dot(a, b, preferred_element_type=F32)


def onehot(hit):
    return jnp.where(hit, 1.0, 0.0).astype(BF)


def spread(ref, expo):
    taps, comps, expos = ref.shape
    named = iota((comps, expos), 1) == expo
    lane = iota((comps, 256), 1) - (128 - taps // 2)
    straight = mirrored = jnp.zeros((comps, 256), F32)
    for t in range(taps):
        tap = jnp.sum(jnp.where(named, ref[t], 0.0), axis=1, keepdims=True)
        straight = jnp.where(lane == t, tap, straight)
        mirrored = jnp.where(lane == taps - 1 - t, tap, mirrored)
    return straight.astype(BF).astype(F32), mirrored.astype(BF).astype(F32)


def bands(base):
    x = jnp.concatenate([base] * 16, axis=0)
    row = iota(x.shape, 0)
    for bit in range(7):
        x = jnp.where((row & (1 << bit)) != 0, pltpu.roll(x, 1 << bit, 1), x)
    return x


def kernel(
    tiles,
    nband,
    cap,
    owner_ref,
    local_ref,
    weight_ref,
    offset_ref,
    expo_ref,
    amp_ref,
    frac_ref,
    sky_hbm,
    obs_hbm,
    col_hbm,
    rowp_hbm,
    total,
    summed_ref,
    sky,
    sky_t,
    obs,
    colp,
    rowp,
    hits,
    picks,
    req_out,
    req_in,
    rows_out,
    rows_in,
    grads_out,
    grads_in,
    card_out,
    cards,
    part_out,
    part_in,
    fet,
    resam,
    base,
    blur,
    fwd,
    bwd,
    tall,
    tall_t,
    obs_t,
    resid,
    back,
    adj,
    seg_grad,
    load_sem,
    req_s,
    req_r,
    rows_s,
    rows_r,
    grads_s,
    grads_r,
    cards_s,
    cards_r,
    part_s,
    part_r,
):
    me = lax.axis_index("tile")
    band = lax.axis_index("band")
    segs, rows = sky.shape
    width = obs.shape[0]
    comps = blur.shape[0]
    pixels = width * rows
    nblk = width // 256
    half = tiles // 2

    loads = [
        pltpu.make_async_copy(src, dst, load_sem.at[i])
        for i, (src, dst) in enumerate(
            ((sky_hbm, sky), (obs_hbm, obs), (col_hbm, colp), (rowp_hbm, rowp))
        )
    ]
    for load in loads:
        load.start()

    barrier = pltpu.get_barrier_semaphore()

    def loop(low, high, work):
        lax.fori_loop(low, high, lambda k, c: (work(k), c)[1], 0)

    loop(
        1,
        tiles,
        lambda k: pl.semaphore_signal(
            barrier, inc=1, device_id={"tile": lax.rem(me + k, tiles)}, device_id_type=MESH
        ),
    )
    loop(
        1,
        nband,
        lambda k: pl.semaphore_signal(
            barrier, inc=1, device_id={"band": lax.rem(band + k, nband)}, device_id_type=MESH
        ),
    )

    inner = lax.rem((me // max(1, tiles // 4) + 1) // 2, 2)

    def peer(step):
        pair = step // 2
        far = 1 - lax.rem(step + inner, 2)
        k = far * (half + pair) + (1 - far) * lax.rem(pair + 1, half)
        bits = [1 << b for b in range(tiles.bit_length() - 1)]
        return sum(lax.rem(me // bit + k // bit, 2) * bit for bit in bits)

    def push(src, dst, send, recv, p):
        return pltpu.make_async_remote_copy(
            src_ref=src.at[p],
            dst_ref=dst.at[me],
            send_sem=send.at[p],
            recv_sem=recv.at[me],
            device_id={"tile": p},
            device_id_type=MESH,
        )

    def arrival(src, dst, send, recv, p):
        return pltpu.make_async_remote_copy(
            src_ref=src.at[p],
            dst_ref=dst.at[p],
            send_sem=send.at[p],
            recv_sem=recv.at[p],
            device_id={"tile": p},
            device_id_type=MESH,
        )

    def deliver(src, dst, send, recv, p):
        @pl.when(p != me)
        def _():
            push(src, dst, send, recv, p).start()

        @pl.when(p == me)
        def _():
            dst[me] = src[me]

    def receive(src, dst, send, recv, p):
        @pl.when(p != me)
        def _():
            arrival(src, dst, send, recv, p).wait_recv()

    owner = owner_ref[...]
    member = jnp.where(iota((tiles, width), 0) == owner, 1.0, 0.0)
    pieces = [member[:, b * 128 : (b + 1) * 128] for b in range(width // 128)]
    above = onehot(iota((128, 128), 0) < iota((128, 128), 1))
    prefix = dot(jnp.concatenate(pieces, axis=0).astype(BF), above)
    run = jnp.zeros((tiles, 1), F32)
    ranks = []
    for b, piece in enumerate(pieces):
        earlier = prefix[b * tiles : (b + 1) * tiles] + run
        ranks.append(jnp.sum(piece * earlier, axis=0, keepdims=True))
        run = run + jnp.sum(piece, axis=1, keepdims=True)
    slot = owner * cap + jnp.concatenate(ranks, axis=1).astype(jnp.int32)
    wanted = local_ref[...] + 1
    which = iota((16, width), 0)
    digits = (
        jnp.where(which == 0, wanted >> 6, jnp.where(which == 1, wanted & 63, 0))
        .astype(F32)
        .astype(BF)
    )
    loads[0].wait()
    for b in range(segs // 128):
        sky_t[:, b * 128 : (b + 1) * 128] = sky[b * 128 : (b + 1) * 128, :].T

    pl.semaphore_wait(barrier, tiles - 1 + nband - 1)

    def ask(step):
        p = peer(step)
        hit = onehot(iota((cap, width), 0) + p * cap == slot)
        hits[p] = hit
        ids = lax.dot_general(digits, hit, NT, preferred_element_type=F32)
        req_out[p] = ids[0:1] * 64.0 + ids[1:2]
        deliver(req_out, req_in, req_s, req_r, p)

    loop(0, tiles, ask)

    keep = cap >= 128

    def pick(p):
        return onehot(iota((segs, cap), 0) + 1 == req_in[p].astype(jnp.int32))

    def serve(step):
        p = peer(step)
        receive(req_out, req_in, req_s, req_r, p)
        chosen = pick(p)
        if keep:
            picks[p] = chosen
        rows_out[p] = dot(sky_t[...], chosen).astype(BF)
        deliver(rows_out, rows_in, rows_s, rows_r, p)

    loop(0, tiles, serve)

    for load in loads[1:]:
        load.wait()
    expo = expo_ref[0, 0]
    offset = offset_ref[0, 0]
    amps = [amp_ref[q, expo] for q in range(comps)]
    for at, made in enumerate((*spread(colp, expo), *spread(rowp, expo))):
        for q in range(comps):
            base[at, q] = jnp.broadcast_to(made[q : q + 1], (8, 256))
    low = iota((128, 128), 1) < 64
    blank = jnp.zeros((128, 128), BF)

    def make_wide(at, wide):
        def work(q):
            made = bands(base[at, q])
            edge, mid = made[:, :128], made[:, 128:].astype(BF)
            left = jnp.where(low, 0.0, edge).astype(BF)
            right = jnp.where(low, edge, 0.0).astype(BF)
            for b, line in enumerate(((right, blank), (mid, right), (left, mid), (blank, left))):
                for h in range(2):
                    wide[q, b * 128 : (b + 1) * 128, h * 128 : (h + 1) * 128] = line[h]

        loop(0, comps, work)

    make_wide(1, fwd)
    make_wide(0, bwd)

    def make_tall(q):
        tall[q] = bands(base[2, q])[:, 128:].astype(BF)
        tall_t[q] = bands(base[3, q])[:, 128:].astype(BF)
        blur[q, :, :128] = blank
        blur[q, :, 128 + width :] = blank

    loop(0, comps, make_tall)
    resid[:, :128] = blank
    resid[:, 128 + width :] = blank
    for b in range(width // 128):
        obs_t[:, b * 128 : (b + 1) * 128] = obs[b * 128 : (b + 1) * 128, :].T
    heavy = jnp.broadcast_to(weight_ref[...], (128, 128)).T
    heavy = jnp.concatenate([heavy, heavy], axis=1)
    frac = jnp.full((128, 128), frac_ref[expo], F32)
    w_low = (1.0 - frac).astype(BF).astype(F32)
    w_high = frac.astype(BF).astype(F32)
    sub, lane = iota((128, 128), 0), iota((128, 128), 1)
    interp_t = (
        jnp.where(lane == sub + offset, w_low, 0.0)
        + jnp.where(lane == sub + offset + 1, w_high, 0.0)
    ).astype(BF)
    interp = (
        jnp.where(sub == lane + offset, w_low, 0.0)
        + jnp.where(sub == lane + offset + 1, w_high, 0.0)
    ).astype(BF)
    slope_t = (
        jnp.where(lane == sub + offset + 1, 1.0, 0.0) - jnp.where(lane == sub + offset, 1.0, 0.0)
    ).astype(BF)

    fet[...] = jnp.zeros_like(fet)

    def take(step):
        p = peer(step)
        receive(rows_out, rows_in, rows_s, rows_r, p)
        fet[...] += dot(rows_in[p], hits[p])

    loop(0, tiles, take)

    resam[...] = dot(interp_t, fet[...].astype(BF)).astype(BF)

    for q in range(comps):
        blur[q, :, 128 : 128 + width] = (amps[q] * dot(tall[q], resam[...])).astype(BF)

    for i in range(nblk):
        model = None
        for q in range(comps):
            part = dot(blur[q, :, i * 256 : i * 256 + 512], fwd[q])
            model = part if model is None else model + part
        weighted = heavy * (model - obs_t[:, i * 256 : (i + 1) * 256].astype(F32))
        resid[:, 128 + i * 256 : 384 + i * 256] = weighted.astype(BF)
    tall_all = jnp.concatenate([tall_t[q] for q in range(comps)], axis=1)
    for i in range(nblk):
        left = resid[:, i * 256 : i * 256 + 512]
        stack = []
        for q in range(comps):
            part = amps[q] * dot(left, bwd[q])
            back[q, :, i * 256 : (i + 1) * 256] = part
            stack.append(part.astype(BF))
        adjoint = dot(tall_all, jnp.concatenate(stack, axis=0))
        adj[:, i * 256 : (i + 1) * 256] = adjoint
        seg_grad[:, i * 256 : (i + 1) * 256] = dot(interp, adjoint.astype(BF)).astype(BF)

    def give(step):
        p = peer(step)
        sent = lax.dot_general(seg_grad[...], hits[p], NT, preferred_element_type=F32)
        grads_out[p] = sent.astype(BF)
        deliver(grads_out, grads_in, grads_s, grads_r, p)

    loop(0, half, give)

    terms = []
    for q in range(comps):
        acc = jnp.sum(blur[q, :, 128 : 128 + width].astype(F32) * back[q], axis=0, keepdims=True)
        gain = jnp.full((1, 1), amps[q], F32)
        terms.append(jnp.sum(acc, axis=1, keepdims=True) / (gain * gain * pixels))
    shift = jnp.sum(adj[...] * dot(slope_t, fet[...].astype(BF)), axis=0, keepdims=True)
    terms.append(jnp.sum(shift, axis=1, keepdims=True) / pixels)

    line = iota((8, 128), 0)
    card = jnp.where(line == 5, expo.astype(F32), 0.0)
    for q, term in enumerate(terms):
        card = jnp.where(line == q, jnp.broadcast_to(term, (8, 128)), card)
    card_out[...] = card
    cards[band] = card

    def swap(k, here):
        to = lax.rem(band + k, nband)
        return pltpu.make_async_remote_copy(
            src_ref=card_out,
            dst_ref=cards.at[band] if here else cards.at[to],
            send_sem=cards_s.at[to],
            recv_sem=cards_r.at[band] if here else cards_r.at[to],
            device_id={"band": to},
            device_id_type=MESH,
        )

    loop(1, nband, lambda k: swap(k, True).start())

    loop(half, tiles, give)

    loop(1, nband, lambda k: swap(k, False).wait_recv())
    expos = summed_ref.shape[1]
    column = iota((8, expos), 1).astype(F32)
    part = jnp.zeros((8, expos), F32)
    for b in range(nband):
        block = jnp.concatenate([cards[b]] * (expos // 128), axis=1)
        part = part + jnp.where(column == block[5:6, :], block, 0.0)
    part_out[...] = part
    part_in[me] = part

    def tell(k, here):
        p = lax.rem(me + k, tiles)
        return pltpu.make_async_remote_copy(
            src_ref=part_out,
            dst_ref=part_in.at[me] if here else part_in.at[p],
            send_sem=part_s.at[p],
            recv_sem=part_r.at[me] if here else part_r.at[p],
            device_id={"tile": p},
            device_id_type=MESH,
        )

    loop(1, tiles, lambda k: tell(k, True).start())

    total[...] = jnp.zeros_like(total)

    def collect(step):
        p = peer(step)
        receive(grads_out, grads_in, grads_s, grads_r, p)
        chosen = picks[p] if keep else pick(p)
        total[...] += lax.dot_general(chosen, grads_in[p], NT, preferred_element_type=F32)

    loop(0, tiles, collect)

    loop(1, tiles, lambda k: tell(k, False).wait_recv())
    summed_ref[...] = lax.fori_loop(
        0, tiles, lambda t, acc: acc + part_in[t], jnp.zeros((8, expos), F32)
    )

    def settle(k):
        p = lax.rem(me + k, tiles)
        push(req_out, req_in, req_s, req_r, p).wait_send()
        push(rows_out, rows_in, rows_s, rows_r, p).wait_send()
        push(grads_out, grads_in, grads_s, grads_r, p).wait_send()
        tell(k, True).wait_send()

    loop(1, tiles, settle)
    loop(1, nband, lambda k: swap(k, True).wait_send())


def finish(total, summed, grad_ref, params_ref, sem):
    pieces = sem.shape[0]
    size = total.shape[0] // pieces
    moves = [
        pltpu.make_async_copy(
            total.at[pl.ds(i * size, size)], grad_ref.at[pl.ds(i * size, size)], sem.at[i]
        )
        for i in range(pieces)
    ]
    for move in moves:
        move.start()
    params_ref[...] = summed[: params_ref.shape[0]]
    for move in moves:
        move.wait()


def body(
    sky_model,
    observed,
    row_weight,
    foot_owner,
    foot_local,
    row_offset,
    exposure_of,
    amplitude,
    subpixel_shift,
    column_profile,
    row_profile,
):
    tiles = lax.axis_size("tile")
    nband = lax.axis_size("band")
    segs, rows = sky_model.shape[1:]
    width = observed.shape[2]
    comps, expos = amplitude.shape
    taps = column_profile.shape[2]
    cap = 2 * width // tiles
    vmem = pl.BlockSpec(memory_space=pltpu.VMEM)
    smem = pl.BlockSpec(memory_space=pltpu.SMEM)
    hbm = pl.BlockSpec(memory_space=pltpu.HBM)
    dma = pltpu.SemaphoreType.DMA
    total, summed = pl.pallas_call(
        functools.partial(kernel, tiles, nband, cap),
        out_shape=(
            jax.ShapeDtypeStruct((segs, rows), F32),
            jax.ShapeDtypeStruct((8, expos), F32),
        ),
        in_specs=[vmem, vmem, vmem, smem, smem, smem, smem, hbm, hbm, hbm, hbm],
        out_specs=(vmem, vmem),
        scratch_shapes=[
            pltpu.VMEM((segs, rows), BF),
            pltpu.VMEM((rows, segs), BF),
            pltpu.VMEM((width, rows), BF),
            pltpu.VMEM((taps, comps, expos), F32),
            pltpu.VMEM((taps, comps, expos), F32),
            pltpu.VMEM((tiles, cap, width), BF),
            pltpu.VMEM((tiles, segs, cap) if cap >= 128 else (16, 128), BF),
            pltpu.VMEM((tiles, 1, cap), F32),
            pltpu.VMEM((tiles, 1, cap), F32),
            pltpu.VMEM((tiles, rows, cap), BF),
            pltpu.VMEM((tiles, rows, cap), BF),
            pltpu.VMEM((tiles, rows, cap), BF),
            pltpu.VMEM((tiles, rows, cap), BF),
            pltpu.VMEM((8, 128), F32),
            pltpu.VMEM((nband, 8, 128), F32),
            pltpu.VMEM((8, expos), F32),
            pltpu.VMEM((tiles, 8, expos), F32),
            pltpu.VMEM((rows, width), F32),
            pltpu.VMEM((rows, width), BF),
            pltpu.VMEM((4, comps, 8, 256), F32),
            pltpu.VMEM((comps, rows, width + 256), BF),
            pltpu.VMEM((comps, 512, 256), BF),
            pltpu.VMEM((comps, 512, 256), BF),
            pltpu.VMEM((comps, rows, rows), BF),
            pltpu.VMEM((comps, rows, rows), BF),
            pltpu.VMEM((rows, width), BF),
            pltpu.VMEM((rows, width + 256), BF),
            pltpu.VMEM((comps, rows, width), F32),
            pltpu.VMEM((rows, width), F32),
            pltpu.VMEM((rows, width), BF),
            dma((4,)),
        ]
        + [dma((tiles,))] * 6
        + [dma((nband,))] * 2
        + [dma((tiles,))] * 2,
        compiler_params=pltpu.CompilerParams(
            collective_id=0, has_side_effects=True, vmem_limit_bytes=60 * 1024 * 1024
        ),
    )(
        foot_owner.reshape(1, width),
        foot_local.reshape(1, width),
        row_weight.reshape(1, rows),
        row_offset,
        exposure_of,
        amplitude,
        subpixel_shift,
        sky_model[0],
        observed[0, 0],
        column_profile.transpose(2, 1, 0),
        row_profile.transpose(2, 1, 0),
    )
    grad, params = pl.pallas_call(
        finish,
        out_shape=(
            jax.ShapeDtypeStruct((segs, rows), F32),
            jax.ShapeDtypeStruct((comps + 1, expos), F32),
        ),
        in_specs=[hbm, vmem],
        out_specs=(hbm, vmem),
        scratch_shapes=[dma((8,))],
        compiler_params=pltpu.CompilerParams(vmem_limit_bytes=60 * 1024 * 1024),
    )(total, summed)
    return (grad[None], params)


def solution(mesh):
    placed = (
        P("band", "tile", None),
        P("band", "tile", None, None),
        P("band", "tile", None),
        P("band", "tile", None, None),
        P("band", "tile", None),
        P("band", "tile"),
        P("band", "tile"),
        P(),
        P(),
        P(),
        P(),
    )
    return jax.shard_map(
        body, mesh=mesh, in_specs=placed, out_specs=(P("band", "tile", None), P()), check_vma=False
    )
```

time: 54 us -> 78.5 us (1.45)
  Pallas kernels: 45.6 us -> 76.3 us
  local copies, waits for them, and re-layouts: 6.02 us -> 0 us
    pallas_call x1, Pallas kernels: 3.04 us -> 34.2 us  [body(): pl.pallas_call(finish, out_shape=(jax.ShapeDtypeStruct((segs, rows), F32)...]
    unnamed x22 -> x0, local copies, waits for them, and re-layouts: 6.02 us -> none
where the time goes in v3:
time: 78.5 us; the launch traced here: 78.2 us
  Pallas kernels  76.3 us (97%)
  between operations  1.93 us (2%)
    pallas_call x1, Pallas kernels, body(): pl.pallas_call(functools.partial(kernel, tiles, nband, cap), out_shape=(j...  42 us
    pallas_call x1, Pallas kernels, body(): pl.pallas_call(finish, out_shape=(jax.ShapeDtypeStruct((segs, rows), F32)...  34.2 us

profile of v3, /device:TPU:0, one launch (start us, length us, event | category | flops | bytes accessed | tf_op | source)
XLA Modules:
  0.0 78.2 jit_solution(16413336101821131266)
XLA Ops:
  1.9 42.0 %shard_map.122 = (f32[2048,128]{1,0:T(8,128)}, f32[8,256]{1,0:T(8,128)}) custom-call(s32[1,1024]{1,0:T(1,128)} %bitcast.12, s32[1,1024]{1,0:T(1,128)} %bitcast.13, f32[1,128]{1,0:T(1,128)} %bitcast.14, s32[1,1]{1,0:T(1,128)S(6)} %copy.13.offset_ref, s32[1,1]{1,0:T(1,128)S(6)} %copy.14.expo_ref, f32[4,256]{1,0:T(4,128)} %amp_ref.1, f32[256]{0:T(256)} %frac_ref.1, ...), custom_call_target="tpu_custom_call" | custom-call | tf_op jit(solution)/shard_map/pallas_call | solution.py:455
  44.0 34.2 %shard_map.123 = (f32[2048,128]{1,0:T(8,128)}, f32[5,256]{1,0:T(8,128)}) custom-call(f32[2048,128]{1,0:T(8,128)} %get-tuple-element.6.total, f32[8,256]{1,0:T(8,128)} %get-tuple-element.7.summed), custom_call_target="tpu_custom_call" | custom-call | tf_op jit(solution)/shard_map/pallas_call | solution.py:515
